TPU v7x, 512 devices: a whole 4x8x8 slice. The times are simulated.
512 devices in a mesh: dp: 4 (over x), width: 16 (over z, core), mlp: 8 (over y).
Axes of the slice: x: 4, y: 8, z: 8, core: 2. Of those that a mesh axis runs over, the one named last changes fastest.
Arguments:
- tokens: bfloat16 [512, 6144], P('dp', 'width'), may hold values from -34 to 34
- gain: float32 [6144], P('width'), may hold values from 0.5 to 1.5
- up_weight: bfloat16 [6144, 12288], P('width', 'mlp'), may hold values from -0.078125 to 0.078125
- down_weight: bfloat16 [12288, 6144], P('mlp', 'width'), may hold values from -0.0546875 to 0.0546875
- cotangent: bfloat16 [512, 6144], P('dp', 'width'), may hold values from -6 to 6
Outputs:
- output: bfloat16 [512, 6144], P('dp', 'width')
- grad_tokens: bfloat16 [512, 6144], P('dp', 'width')
- grad_gain: float32 [6144], P('width')
- grad_up: float32 [6144, 8, 1536], P('width', 'mlp', 'dp')
- grad_down: float32 [8, 1536, 6144], P('mlp', 'dp', 'width')
All inputs are finite; a program needn't handle non-finite values.
Results may differ from a plain program's by a relative error of at most 0.025.
Values may be sent and summed in bfloat16 or wider, within the bound.
A program may use at most 64 MiB of HBM per device.

v0:
```python
import jax
import jax.numpy as jnp
from jax import lax
from jax.sharding import PartitionSpec as P

D = 6144


inv_root_two = 0.7071067811865476
inv_root_two_pi = 0.3989422804014327


def gelu_value(values):
    return 0.5 * values * (1.0 + lax.erf(values * inv_root_two))


def gelu_slope(values):
    return (
        0.5 * (1.0 + lax.erf(values * inv_root_two))
        + values * jnp.exp(-0.5 * values * values) * inv_root_two_pi
    )


def contract(left, right, left_dim, right_dim):
    return lax.dot_general(
        left, right, (((left_dim,), (right_dim,)), ((), ())), preferred_element_type=jnp.float32
    )


def shards(tokens, gain, up_weight, down_weight, cotangent):
    inputs = tokens.astype(jnp.float32)
    token_sums = lax.psum(jnp.sum(inputs, axis=1), "width")
    mean_all = token_sums / D
    shifted = inputs - mean_all[:, None]
    variance = lax.psum(jnp.sum(shifted * shifted, axis=1), "width") / D
    inv_std = lax.rsqrt(variance + 1e-06)
    normed = (inputs - mean_all[:, None]) * inv_std[:, None]
    scaled = (normed * gain[None, :]).astype(jnp.bfloat16)
    rows = scaled
    pre_act = lax.psum_scatter(
        jnp.dot(rows, up_weight, preferred_element_type=jnp.float32).astype(jnp.bfloat16),
        "width",
        scatter_dimension=0,
        tiled=True,
    ).astype(jnp.float32)
    hidden = gelu_value(pre_act).astype(jnp.bfloat16)
    hidden_all = lax.all_gather(hidden, "width", axis=0, tiled=True)
    partial_out = jnp.dot(hidden_all, down_weight, preferred_element_type=jnp.float32)
    rows = cotangent
    grad_hidden = lax.psum_scatter(
        contract(rows, down_weight, 1, 1).astype(jnp.bfloat16),
        "width",
        scatter_dimension=0,
        tiled=True,
    ).astype(jnp.float32)
    grad_pre = (grad_hidden * gelu_slope(pre_act)).astype(jnp.bfloat16)
    grad_pre_all = lax.all_gather(grad_pre, "width", axis=0, tiled=True)
    partial_grad = contract(grad_pre_all, up_weight, 1, 1)
    output = lax.psum(partial_out.astype(jnp.bfloat16), "mlp")
    grad_scaled = lax.psum(partial_grad.astype(jnp.bfloat16), "mlp").astype(jnp.float32)
    grad_normed = grad_scaled * gain[None, :]
    first_sum, second_sum = lax.psum(
        (jnp.sum(grad_normed, axis=1), jnp.sum(grad_normed * normed, axis=1)), "width"
    )
    grad_tokens = (
        inv_std[:, None]
        * (grad_normed - first_sum[:, None] / D - normed * (second_sum[:, None] / D))
    ).astype(jnp.bfloat16)
    grad_gain = lax.psum(jnp.sum(grad_scaled * normed, axis=0), "dp")
    up_grad = contract(scaled, grad_pre_all, 0, 0)
    down_grad_flip = contract(cotangent, hidden_all, 0, 0)
    up_share, down_share = (
        lax.psum_scatter(
            up_grad.astype(jnp.bfloat16), "dp", scatter_dimension=1, tiled=True
        ).astype(jnp.float32),
        lax.psum_scatter(
            down_grad_flip.astype(jnp.bfloat16), "dp", scatter_dimension=1, tiled=True
        ).astype(jnp.float32),
    )
    grad_up = up_share[:, None, :]
    grad_down = jnp.transpose(down_share)[None, :, :]
    return (output, grad_tokens, grad_gain, grad_up, grad_down)


def solution(mesh):
    placed = (P("dp", "width"), P("width"), P("width", "mlp"), P("mlp", "width"), P("dp", "width"))
    return jax.shard_map(
        shards,
        mesh=mesh,
        in_specs=placed,
        out_specs=(
            P("dp", "width"),
            P("dp", "width"),
            P("width"),
            P("width", "mlp", "dp"),
            P("mlp", "dp", "width"),
        ),
        check_vma=False,
    )
```

profile of v0, /device:TPU:1, one launch (start us, length us, event | category | flops | bytes accessed | tf_op | source)
XLA Modules:
  0.0 367.4 jit_solution(14303071194060131388)
XLA Ops:
  7.2 0.0 copy-start
  7.2 0.0 copy-start.3
  7.2 0.0 copy-start.1
  7.2 0.0 reduce-scatter.7.cloned.1.call-start
  7.2 1.1 convert_reduce_fusion
  8.4 30.6 %psum.49 = f32[128]{0:T(128)S(1)} all-reduce(f32[128]{0:T(128)S(1)} %convert_reduce_fusion), channel_id=1, replica_groups=mesh['dp'=4,'width'=16,'mlp'=8] {'width'}, use_global_device_ids=true, to_apply=%region_1.0 | all-reduce | flops 128 | bytes 1024 | tf_op jit(solution)/shard_map/psum | solution.py:32
  39.0 1.1 fusion.12
  40.1 25.8 %psum.50 = f32[128]{0:T(128)S(1)} all-reduce(f32[128]{0:T(128)S(1)} %fusion.12), channel_id=1, replica_groups=mesh['dp'=4,'width'=16,'mlp'=8] {'width'}, use_global_device_ids=true, to_apply=%region_3.0 | all-reduce | flops 128 | bytes 1024 | tf_op jit(solution)/shard_map/psum | solution.py:35
  65.9 0.0 copy-done
  65.9 2.1 convolution_convert_fusion.3
  68.0 0.0 reduce-scatter.7.cloned.1.call-update
  68.0 0.0 reduce-scatter.9.cloned.1.call-start
  68.1 0.0 copy-done.3
  68.1 0.0 copy-done.1
  68.1 1.3 convolution_convert_fusion.2
  69.3 0.0 reduce-scatter.9.cloned.1.call-update
  69.4 0.0 all-reduce.4.cloned.1.call-start
  69.4 51.8 %reduce-scatter.7.cloned.1.call-done = bf16[8,1536]{1,0:T(8,128)(2,1)} async-done(((bf16[128,1536]{1,0:T(8,128)(2,1)}), bf16[8,1536]{1,0:T(8,128)(2,1)}) %reduce-scatter.7.cloned.1.call-update) | async-done | bytes 24592 | tf_op jit(solution)/shard_map/reduce_scatter | solution.py:40
  121.3 61.3 %reduce-scatter.9.cloned.1.call-done = bf16[8,1536]{1,0:T(8,128)(2,1)} async-done(((bf16[128,1536]{1,0:T(8,128)(2,1)}), bf16[8,1536]{1,0:T(8,128)(2,1)}) %reduce-scatter.9.cloned.1.call-update) | async-done | bytes 24592 | tf_op jit(solution)/shard_map/reduce_scatter | solution.py:50
  182.5 0.8 fusion.23
  183.3 18.6 %all_gather.7 = bf16[128,1536]{1,0:T(8,128)(2,1)S(1)} all-gather(bf16[8,1536]{1,0:T(8,128)(2,1)S(1)} %get-tuple-element.22), channel_id=1, replica_groups=mesh['dp'=4,'width'=16,'mlp'=8] {'width'}, dimensions={0}, use_global_device_ids=true | all-gather | bytes 417792 | tf_op jit(solution)/shard_map/all_gather | solution.py:57
  201.9 1.2 convolution_convert_fusion.4
  203.0 0.0 copy-start.2
  203.0 0.0 copy-start.5
  203.0 17.2 %all_gather.6 = bf16[128,1536]{1,0:T(8,128)(2,1)S(1)} all-gather(bf16[8,1536]{1,0:T(8,128)(2,1)S(1)} %get-tuple-element.23), channel_id=1, replica_groups=mesh['dp'=4,'width'=16,'mlp'=8] {'width'}, dimensions={0}, use_global_device_ids=true | all-gather | bytes 417792 | tf_op jit(solution)/shard_map/all_gather | solution.py:47
  220.3 1.0 convolution_convert_fusion.5
  221.3 0.0 all-reduce.4.cloned.1.call-update
  221.3 0.0 reduce-scatter.13.cloned.1.call-start
  221.4 0.0 copy-done.2
  221.4 0.0 copy-done.5
  221.4 0.6 convolution_convert_fusion.1
  222.0 1.4 copy.12
  223.4 0.0 reduce-scatter.13.cloned.1.call-update
  223.4 0.0 reduce-scatter.11.cloned.1.call-start
  223.5 1.6 fusion
  225.0 0.0 reduce-scatter.11.cloned.1.call-update
  225.0 66.3 %all-reduce.4.cloned.1.call-done = (bf16[128,384]{1,0:T(8,128)(2,1)}, bf16[128,384]{1,0:T(8,128)(2,1)}) async-done(((bf16[128,384]{1,0:T(8,128)(2,1)}, bf16[128,384]{1,0:T(8,128)(2,1)}), (bf16[128,384]{1,0:T(8,128)(2,1)}, bf16[128,384]{1,0:T(8,128)(2,1)})) %all-reduce.4.cloned.1.call-update) | async-done | bytes 196624 | tf_op jit(solution)/shard_map/psum | solution.py:59
  291.4 1.1 fusion.14
  292.5 30.0 %all-reduce = (f32[128]{0:T(128)S(1)}, f32[128]{0:T(128)S(1)}) all-reduce(f32[128]{0:T(128)S(1)} %get-tuple-element.16, f32[128]{0:T(128)S(1)} %get-tuple-element.17), channel_id=1, replica_groups=mesh['dp'=4,'width'=16,'mlp'=8] {'width'}, use_global_device_ids=true, to_apply=%region_11.0 | all-reduce | flops 256 | bytes 2048 | tf_op jit(solution)/shard_map/psum | solution.py:62
  322.5 9.0 %psum.55 = f32[384]{0:T(512)} all-reduce(f32[384]{0:T(512)S(1)} %get-tuple-element.15), channel_id=1, replica_groups=mesh['dp'=4,'width'=16,'mlp'=8] {'dp'}, use_global_device_ids=true, to_apply=%region_13.0 | all-reduce | flops 384 | bytes 3072 | tf_op jit(solution)/shard_map/psum | solution.py:69
  331.4 1.7 fusion.11
  333.1 0.0 reduce-scatter.13.cloned.1.call-done
  333.1 1.2 copy.13
  334.3 0.0 copy-start.4
  334.3 1.4 copy.11
  335.8 22.6 %reduce-scatter.11.cloned.1.call-done = bf16[384,384]{0,1:T(8,128)(2,1)} async-done(((bf16[384,1536]{0,1:T(8,128)(2,1)}), bf16[384,384]{0,1:T(8,128)(2,1)}) %reduce-scatter.11.cloned.1.call-update) | async-done | bytes 294928 | tf_op jit(solution)/shard_map/reduce_scatter | solution.py:76
  358.4 1.8 convert_bitcast_fusion
  360.2 0.0 copy-done.4
  360.2 0.6 copy.16
  (4 shorter events, 0.1 us)
Async XLA Ops:
  7.2 58.7 %copy-start = (bf16[384,1536]{1,0:T(8,128)(2,1)S(1)}, bf16[384,1536]{1,0:T(8,128)(2,1)}, u32[]{:S(2)}) copy-start(bf16[384,1536]{1,0:T(8,128)(2,1)} %param.7) | copy-start | bytes 3538948
  7.2 60.9 %copy-start.3 = (bf16[128,384]{1,0:T(8,128)(2,1)S(1)}, bf16[128,384]{1,0:T(8,128)(2,1)}, u32[]{:S(2)}) copy-start(bf16[128,384]{1,0:T(8,128)(2,1)} %param.9) | copy-start | bytes 294916
  7.2 60.9 %copy-start.1 = (bf16[1536,384]{1,0:T(8,128)(2,1)S(1)}, bf16[1536,384]{1,0:T(8,128)(2,1)}, u32[]{:S(2)}) copy-start(bf16[1536,384]{1,0:T(8,128)(2,1)} %param.8) | copy-start | bytes 3538948
  7.2 114.0 %reduce-scatter.7.cloned.1.call-start = ((), (), s32[]{:S(2)}) async-start(), calls=%async_computation.4 | async-start | bytes 417792 | tf_op jit(solution)/shard_map/reduce_scatter | solution.py:40
  68.0 114.5 %reduce-scatter.9.cloned.1.call-start = ((), (), s32[]{:S(2)}) async-start(), calls=%async_computation.5 | async-start | bytes 417792 | tf_op jit(solution)/shard_map/reduce_scatter | solution.py:50
  69.4 222.0 %all-reduce.4.cloned.1.call-start = ((), (), s32[]{:S(2)}) async-start(), calls=%async_computation.8 | async-start | bytes 393216 | tf_op jit(solution)/shard_map/psum | solution.py:59
  203.0 18.3 %copy-start.2 = (bf16[128,384]{1,0:T(8,128)(2,1)S(1)}, bf16[128,384]{1,0:T(8,128)(2,1)}, u32[]{:S(2)}) copy-start(bf16[128,384]{1,0:T(8,128)(2,1)} %param.5) | copy-start | bytes 294916
  203.0 18.3 %copy-start.5 = (f32[384]{0:T(512)S(1)}, f32[384]{0:T(512)}, u32[]{:S(2)}) copy-start(f32[384]{0:T(512)} %param.6) | copy-start | bytes 4612
  221.3 111.8 %reduce-scatter.13.cloned.1.call-start = ((), (), s32[]{:S(2)}) async-start(), calls=%async_computation.7 | async-start | bytes 1474560
  223.4 135.0 %reduce-scatter.11.cloned.1.call-start = ((), (), s32[]{:S(2)}) async-start(), calls=%async_computation.6 | async-start | bytes 1474560 | tf_op jit(solution)/shard_map/reduce_scatter | solution.py:76
  334.3 25.9 %copy-start.4 = (bf16[128,384]{1,0:T(8,128)(2,1)S(1)}, bf16[128,384]{1,0:T(8,128)(2,1)}, u32[]{:S(2)}) copy-start(bf16[128,384]{1,0:T(8,128)(2,1)} %get-tuple-element.26) | copy-start | bytes 294916
Sparse Core Ops, SparseCore 0:
  68.1 53.0 reduce-scatter.6
  124.8 57.6 reduce-scatter.8
  221.5 69.8 all-reduce.3
  294.3 31.8 reduce-scatter.12
  329.2 29.1 reduce-scatter.10
where the time goes:
time: 368 us; the launch traced here: 367 us
  waiting for transfers between devices  202 us (55%)
  blocking collectives  131 us (36%)
  between operations  13.9 us (4%)
  other arithmetic  7.64 us (2%)
  matrix products  7.63 us (2%)
  local copies, waits for them, and re-layouts  4.66 us (1%)
    psum x1, waiting for transfers between devices, shards(): output = lax.psum(partial_out.astype(jnp.bfloat16), 'mlp')  66.3 us
    reduce_scatter x1, waiting for transfers between devices, shards(): lax.psum_scatter(contract(rows, down_weight, 1, 1).astype(jnp.bfloat16),...  61.3 us
    reduce_scatter x1, waiting for transfers between devices, shards(): lax.psum_scatter(jnp.dot(rows, up_weight, preferred_element_type=jnp.floa...  51.8 us
    psum x1, blocking collectives, shards(): token_sums = lax.psum(jnp.sum(inputs, axis=1), 'width')  30.6 us
    psum x1, blocking collectives, shards(): lax.psum((jnp.sum(grad_normed, axis=1), jnp.sum(grad_normed * normed, axi...  30 us
    psum x1, blocking collectives, shards(): variance = lax.psum(jnp.sum(shifted * shifted, axis=1), 'width') / D  25.8 us
    reduce_scatter x1, waiting for transfers between devices, shards(): lax.psum_scatter(down_grad_flip.astype(jnp.bfloat16), 'dp', scatter_dimen...  22.6 us
    all_gather x1, blocking collectives, shards(): grad_pre_all = lax.all_gather(grad_pre, 'width', axis=0, tiled=True)  18.6 us
  transfers between devices with their start and end apart: 5, of which 4 were waited for; matrix products, arithmetic and copies ran while one was open for 3% of the time, Pallas kernels for 0%

commit v1 on v0

v1 whole, which is shorter than its diff:
```python
import functools

import jax
import jax.numpy as jnp
from jax import lax
from jax.experimental import pallas as pl
from jax.experimental.pallas import tpu as pltpu
from jax.sharding import PartitionSpec as P

MESH = pl.DeviceIdType.MESH
F32, BF16 = jnp.float32, jnp.bfloat16
TB = 16
EXTRA = 128

inv_root_two = 0.7071067811865476
inv_root_two_pi = 0.3989422804014327


def dot(left, right, left_dim, right_dim):
    return lax.dot_general(
        left, right, (((left_dim,), (right_dim,)), ((), ())), preferred_element_type=F32
    )


def pack(first, second):
    lane = lax.broadcasted_iota(jnp.int32, (first.shape[0], EXTRA), 1)
    high_one, high_two = first.astype(BF16).astype(F32), second.astype(BF16).astype(F32)
    held = jnp.where(lane == 0, high_one, 0.0)
    held = jnp.where(lane == 1, high_two, held)
    held = jnp.where(lane == 2, first - high_one, held)
    held = jnp.where(lane == 3, second - high_two, held)
    return held.astype(BF16)


def unpack(held):
    return held[:, 0:1] + held[:, 2:3], held[:, 1:2] + held[:, 3:4]


def send(src, dst, ss, rs, **where):
    pltpu.make_async_remote_copy(
        src_ref=src, dst_ref=dst, send_sem=ss, recv_sem=rs, device_id=where, device_id_type=MESH
    ).start()


def arrived(ref, sem):
    pltpu.make_async_copy(ref, ref, sem).wait()


def ring(axis, me, device=lambda position: position):
    def at(o):
        return lax.rem(me + o % 8, 8)
    return at, lambda o: {axis: device(at(o))}


def lanes_of(block, side):
    cut = block.shape[-1] // 256 * 128
    return block.at[:, pl.ds(0, cut) if side == 0 else pl.ds(cut, block.shape[-1] - cut)]


def scatter(to_whom, terms, got, halves, ss, rs):
    at, to = to_whom
    for side, o in ((0, 1), (1, -1)):
        send(terms.at[at(3 * o)], got.at[4 + side], ss, rs.at[4 + side], **to(o))
    for side, o in ((0, 2), (1, -2)):
        send(lanes_of(terms.at[at(4)], side), halves[side], ss, rs.at[6 + side], **to(o))
    for side, o in ((0, 1), (1, -1)):
        send(terms.at[at(o)], got.at[side], ss, rs.at[side], **to(o))


def scatter_pass(to_whom, own, got, halves, sums, ss, rs):
    at, to = to_whom
    for side, o in ((0, 2), (1, -2)):
        arrived(got.at[4 + side], rs.at[4 + side])
        arrived(halves[side], rs.at[6 + side])
        term = own[at(o)] + got[4 + side].astype(F32)
        half = halves[side][...].astype(F32)
        cut = term.shape[-1] // 256 * 128
        low, high = term[:, 0:cut], term[:, cut:]
        sums[side, :, 0:cut] = (low + half if side == 0 else low).astype(BF16)
        sums[side, :, cut:] = (high if side == 0 else high + half).astype(BF16)
        send(sums.at[side], got.at[2 + side], ss, rs.at[2 + side], **to(o))


def scatter_sum(to_whom, own, got, rs):
    at, _ = to_whom
    for slot in range(4):
        arrived(got.at[slot], rs.at[slot])
    return own[at(0)] + jnp.sum(got[0:4].astype(F32), axis=0)


def gather(to_whom, buf, ss, rs):
    at, to = to_whom
    block = buf.at[at(0)]
    for o, slot in ((2, 2), (-2, 3), (1, 0), (-1, 1)):
        send(block, block, ss, rs.at[slot], **to(o))


def gather_pass(here, there, buf, ss, rs, far_rs, use):
    at, _ = here
    for side, o in ((0, 1), (1, -1)):
        block = buf.at[at(-2 * o)]
        arrived(block, rs.at[2 + side])
        half = lanes_of(block, side)
        for (_, to), sems, first in ((here, rs, 4), (there, far_rs, 0)):
            send(block, block, ss, sems.at[first + side], **to(o))
            send(half, half, ss, sems.at[first + 2 + side], **to(2 * o))
        use(block)


def gather_near(here, buf, rs, use):
    at, _ = here
    for side, o in ((0, -1), (1, 1)):
        arrived(buf.at[at(o)], rs.at[side])
        use(buf.at[at(o)])


def gather_far(here, buf, sems, first):
    at, _ = here
    for side, o in ((0, -3), (1, 3)):
        arrived(buf.at[at(o)], sems.at[first + side])
        arrived(lanes_of(buf.at[at(4)], side), sems.at[first + 2 + side])


def around(i, n):
    half = lax.div(n - 2 - i, 2) + 1
    return jnp.where(lax.rem(n - 2 - i, 2) == 0, half, n - half)


def direct_scatter(axis, me, n, terms, got, ss, rs):
    def one(i, carry):
        o = around(i, n)
        peer = lax.rem(me + o, n)
        send(terms.at[peer], got.at[o - 1], ss, rs, **{axis: peer})
        return carry
    lax.fori_loop(0, n - 1, one, 0)


def direct_gather(axis, me, n, buf, ss, rs):
    def one(i, carry):
        send(buf.at[me], buf.at[me], ss, rs, **{axis: lax.rem(me + around(i, n), n)})
        return carry
    lax.fori_loop(0, n - 1, one, 0)


def kernel(
    sizes, tok_h, gain_h, wup_h, wdn_h, cot_h, out, gt, gg, gup, gdn,
    tok, gain_v, wup, wdn, cotx, scx, normed, inv_col,
    stat_s, stat_r,
    sib_s, sib_r, own, zs, zr, zh, zc, leaning, away_col,
    hid, gp, hx, gpx,
    ys0, yr0, part0, ys1, yr1, part1,
    outv, gtv,
    gg_s, ggx_r, ggy_s, ggy_r,
    ld, sib_ss, sib_rs, stat_ss, stat_rs, z_ss, z_rs, ag_ss, ag_rs, far_rs, rel_ss, rel_rs,
    x_ss, x_rs, q_ss, q_rs, join_ss, join_rs, y_ss, y_rs, yag_ss, yag_rs, ggx_ss, ggx_rs, ggy_ss, ggy_rs,
):
    NX, NZ, NY, D = sizes
    T, DS = tok.shape
    TY = T // NY
    FS = wup.shape[1]
    FH, FQ = FS // 2, FS // NX
    NW = 2 * NZ
    x, w, y = lax.axis_index("dp"), lax.axis_index("width"), lax.axis_index("mlp")
    z = lax.div(w, 2)
    c = w - 2 * z
    sibling = 2 * z + 1 - c

    over_z = ring("width", z, lambda position: 2 * position + c)
    across_z = ring("width", z, lambda position: 2 * position + 1 - c)

    def quarter(q):
        first = q * FQ
        h = lax.div(first, FH)
        return h, pl.ds(pl.multiple_of(first - h * FH, FQ), FQ)

    loads = [
        pltpu.make_async_copy(tok_h, tok, ld.at[0]),
        pltpu.make_async_copy(gain_h, gain_v, ld.at[1]),
        pltpu.make_async_copy(wup_h, wup, ld.at[2]),
        pltpu.make_async_copy(cot_h, cotx.at[0], ld.at[3]),
        pltpu.make_async_copy(wdn_h, wdn, ld.at[4]),
    ]
    for load in loads:
        load.start()

    barrier = pltpu.get_barrier_semaphore()

    def greet(axis, me, n):
        def one(k, carry):
            pl.semaphore_signal(barrier, inc=1, device_id={axis: lax.rem(me + k, n)}, device_id_type=MESH)
            return carry
        lax.fori_loop(1, n, one, 0)

    greet("width", w, NW)
    greet("mlp", y, NY)
    greet("dp", x, NX)

    mine = pl.ds(pl.multiple_of(c * FH, FH), FH)
    other = pl.ds(pl.multiple_of(FH - c * FH, FH), FH)

    loads[0].wait()
    loads[1].wait()
    values = tok[...].astype(F32)
    total = jnp.sum(values, axis=1, keepdims=True)
    shifted = values - total * (1.0 / DS)
    spread = jnp.sum(shifted * shifted, axis=1, keepdims=True)
    g_all = gain_v[...].reshape(1, DS)
    leaning[0:T] = (shifted * g_all).astype(BF16)
    row = lax.broadcasted_iota(jnp.int32, (TB, DS), 0)
    g_one = g_all.astype(BF16).astype(F32)
    g_two = (g_all - g_one).astype(BF16).astype(F32)
    g_rows = jnp.where(row == 0, g_one, jnp.where(row == 1, g_two, jnp.where(row == 2, g_all - g_one - g_two, 0.0)))
    leaning[T:] = g_rows.astype(BF16)
    loads[2].wait()
    its_half = dot(leaning[...], wup[:, other], 1, 0)
    sib_s[0] = its_half[0:T].astype(BF16)
    pl.semaphore_wait(barrier, NW - 1 + NY - 1 + NX - 1)
    send(sib_s.at[0], sib_r.at[0], sib_ss.at[0], sib_rs.at[0], width=sibling)

    loads[3].wait()
    loads[4].wait()
    sib_s[1] = dot(cotx[0], wdn[other, :], 1, 1).astype(BF16)
    send(sib_s.at[1], sib_r.at[1], sib_ss.at[1], sib_rs.at[1], width=sibling)

    def merge(k, mine_half):
        arrived(sib_r.at[k], sib_rs.at[k])
        both = (mine_half + sib_r[k].astype(F32)).reshape(NZ, TB, FH)
        own[k] = both
        zs[k] = both.astype(BF16)
        scatter(over_z, zs.at[k], zr.at[k], [zh.at[k, 0], zh.at[k, 1]], z_ss.at[k], z_rs.at[k])

    def merge_pass(k):
        scatter_pass(
            over_z, own.at[k], zr.at[k], [zh.at[k, 0], zh.at[k, 1]], zc.at[k], z_ss.at[k], z_rs.at[k]
        )

    my_half = dot(leaning[...], wup[:, mine], 1, 0)
    merge(0, my_half[0:T])
    merge(1, dot(cotx[0], wdn[mine, :], 1, 1))

    total_row = jnp.transpose(jnp.broadcast_to(total, (T, EXTRA)))[0:1]
    spread_row = jnp.transpose(jnp.broadcast_to(spread, (T, EXTRA)))[0:1]
    for h, half in ((c, my_half), (1 - c, its_half)):
        lean = jnp.sum(half[T:], axis=0, keepdims=True)
        stat_s[h, 0:1, 0:T] = total_row
        stat_s[h, 1:2, 0:T] = spread_row
        for j in range(FH // 128):
            stat_s[h, 2 + j : 3 + j, :] = lean[:, j * 128 : (j + 1) * 128]

    def tell(k, carry):
        peer = lax.rem(w + k, NW)
        send(stat_s.at[lax.rem(peer, 2)], stat_r.at[k - 1], stat_ss, stat_rs, width=peer)
        return carry
    lax.fori_loop(1, NW, tell, 0)

    right, left = lax.rem(x + 1, NX), lax.rem(x + NX - 1, NX)
    first_rows, last_rows = pl.ds(0, T // 2), pl.ds(T // 2, T // 2)

    def spread_x(k, buf):
        send(buf.at[0], buf.at[1], x_ss.at[k], x_rs.at[k, 0], dp=right)
        send(buf.at[0], buf.at[NX - 1], x_ss.at[k], x_rs.at[k, 1], dp=left)

    def pass_x(k, buf):
        arrived(buf.at[1], x_rs.at[k, 0])
        send(buf.at[1, first_rows], buf.at[2, first_rows], x_ss.at[k], x_rs.at[k, 2], dp=right)
        arrived(buf.at[NX - 1], x_rs.at[k, 1])
        send(buf.at[NX - 1, last_rows], buf.at[2, last_rows], x_ss.at[k], x_rs.at[k, 3], dp=left)

    def end_x(k, buf):
        arrived(buf.at[2, first_rows], x_rs.at[k, 2])
        arrived(buf.at[2, last_rows], x_rs.at[k, 3])

    merge_pass(0)
    merge_pass(1)
    spread_x(0, cotx)

    arrived(stat_r, stat_rs)
    its = stat_r[...]
    my_stat = stat_s[c]
    sums, spreads = its[:, 0, :], its[:, 1, :]
    mean = (jnp.sum(sums, axis=0, keepdims=True) + my_stat[0:1]) * (1.0 / D)
    away, my_away = sums * (1.0 / DS) - mean, my_stat[0:1] * (1.0 / DS) - mean
    variance = (
        jnp.sum(spreads + DS * away * away, axis=0, keepdims=True) + my_stat[1:2] + DS * my_away * my_away
    ) * (1.0 / D)
    inv_std = lax.rsqrt(variance + 1e-06)
    mean_col = jnp.transpose(jnp.broadcast_to(mean[:, 0:T], (EXTRA, T)))
    std_col = jnp.transpose(jnp.broadcast_to(inv_std[:, 0:T], (EXTRA, T)))
    inv_col[...] = std_col
    aways = jnp.concatenate([away[:, 0:T], my_away[:, 0:T], jnp.zeros((EXTRA - NW, T), F32)], axis=0)
    away_col[...] = jnp.transpose(aways)
    token_rows = pl.ds(pl.multiple_of(z * TB, TB), TB)
    my_aways = away_col[token_rows, :]
    leans, shift = [], []
    for j in range(FH // 128):
        piece = [its[s, 2 + j : 3 + j, :] for s in range(NW - 1)] + [my_stat[2 + j : 3 + j, :]]
        leans.append(functools.reduce(jnp.add, piece))
        shift.append(functools.reduce(jnp.add, [my_aways[:, s : s + 1] * piece[s] for s in range(NW)]))
    lean_row = jnp.concatenate(leans, axis=1)
    shift = jnp.concatenate(shift, axis=1)
    def hand_over(k):
        return lambda block: send(block, block, rel_ss.at[k], rel_rs.at[k], width=sibling)

    pre_act = (scatter_sum(over_z, own.at[0], zr.at[0], z_rs.at[0]) + shift) * inv_col[token_rows, 0:1]
    below = 0.5 * (1.0 + lax.erf(pre_act * inv_root_two))
    hid[c, z] = (pre_act * below).astype(BF16)
    units, grads = hid.at[c], gp.at[c]
    gather(over_z, units, ag_ss.at[0], ag_rs.at[0])
    hand_over(0)(hid.at[c, z])
    slope = below + pre_act * jnp.exp(-0.5 * pre_act * pre_act) * inv_root_two_pi
    grad_hidden = scatter_sum(over_z, own.at[1], zr.at[1], z_rs.at[1])
    grad_pre = (grad_hidden * slope).astype(BF16)
    wide = grad_pre.astype(F32)
    gp[c, z, :, 0:FH] = grad_pre
    gp[c, z, :, FH:] = pack(
        jnp.sum(wide * lean_row, axis=1, keepdims=True), jnp.sum(wide * pre_act, axis=1, keepdims=True)
    )
    gather(over_z, grads, ag_ss.at[1], ag_rs.at[1])
    hand_over(1)(gp.at[c, z])

    gather_pass(over_z, across_z, units, ag_ss.at[0], ag_rs.at[0], far_rs.at[0], hand_over(0))
    gather_near(over_z, units, ag_rs.at[0], hand_over(0))
    gather_pass(over_z, across_z, grads, ag_ss.at[1], ag_rs.at[1], far_rs.at[1], hand_over(1))
    gather_near(over_z, grads, ag_rs.at[1], hand_over(1))
    pass_x(0, cotx)
    for j in range(DS // 128):
        cols = slice(j * 128, (j + 1) * 128)
        normal = (tok[:, cols].astype(F32) - mean_col) * std_col
        normed[:, cols] = normal
        scx[0, :, cols] = (normal * g_all[:, cols]).astype(BF16)
    spread_x(1, scx)

    def gathered(k, buf):
        gather_far(over_z, buf.at[c], ag_rs.at[k], 4)
        gather_far(over_z, buf.at[1 - c], far_rs.at[k], 0)
        arrived(buf.at[1 - c, pl.ds(0, 5)], rel_rs.at[k])

    gathered(0, hid)

    term = dot(hid[0].reshape(T, FH), wdn[0:FH, :], 1, 0) + dot(hid[1].reshape(T, FH), wdn[FH:, :], 1, 0)
    term = term.reshape(NY, TY, DS)
    part0[...] = term
    ys0[...] = term.astype(BF16)
    direct_scatter("mlp", y, NY, ys0, yr0, y_ss.at[0], y_rs.at[0])

    my_blocks = pl.ds(pl.multiple_of(c * (NZ // 2), NZ // 2), NZ // 2)
    its_blocks = pl.ds(pl.multiple_of((1 - c) * (NZ // 2), NZ // 2), NZ // 2)

    def share(k, buf, dst):
        def one(o, carry):
            peer = lax.rem(x + o, NX)
            h, lanes = quarter(peer)
            send(buf.at[h, my_blocks, :, lanes], dst.at[o, my_blocks], q_ss.at[k], q_rs.at[k], dp=peer)
            return carry
        lax.fori_loop(1, NX, one, 0)
        h, lanes = quarter(x)
        dst[0] = buf[h, :, :, lanes]

    def join(k, dst):
        halves = dst.at[pl.ds(1, NX - 1), my_blocks]
        arrived(halves, q_rs.at[k])
        send(halves, halves, join_ss.at[k], join_rs.at[k], width=sibling)

    share(0, hid, hx)

    gathered(1, gp)
    term = dot(gp[0, :, :, 0:FH].reshape(T, FH), wup[:, 0:FH], 1, 1) + dot(
        gp[1, :, :, 0:FH].reshape(T, FH), wup[:, FH:], 1, 1
    )
    side = (gp[0, :, :, FH:].astype(F32) + gp[1, :, :, FH:].astype(F32)).reshape(T, EXTRA)
    part1[:, :, 0:DS] = term.reshape(NY, TY, DS)
    ys1[:, :, 0:DS] = term.reshape(NY, TY, DS).astype(BF16)
    part1[:, :, DS:] = side.reshape(NY, TY, EXTRA)
    ys1[:, :, DS:] = pack(*unpack(side)).reshape(NY, TY, EXTRA)
    direct_scatter("mlp", y, NY, ys1, yr1, y_ss.at[1], y_rs.at[1])
    share(1, gp, gpx)
    pass_x(1, scx)
    join(0, hx)

    arrived(yr0, y_rs.at[0])
    outv[y] = (part0[y] + jnp.sum(yr0[...].astype(F32), axis=0)).astype(BF16)
    direct_gather("mlp", y, NY, outv, yag_ss.at[0], yag_rs.at[0])

    end_x(0, cotx)
    arrived(hx.at[pl.ds(1, NX - 1), its_blocks], join_rs.at[0])
    gdn[...] = dot(hx[...].reshape(NX * T, FQ), cotx[...].reshape(NX * T, DS), 0, 0)
    arrived(yr1, y_rs.at[1])
    whole = part1[y] + jnp.sum(yr1[...].astype(F32), axis=0)
    grad_scaled = whole[:, 0:DS]
    first, second = unpack(whole[:, DS:])
    block = pl.ds(pl.multiple_of(y * TY, TY), TY)
    normal = normed[block, :]
    gtv[y] = (
        inv_col[block, 0:1] * (grad_scaled * gain_v[...].reshape(1, DS) - first * (1.0 / D) - normal * (second * (1.0 / D)))
    ).astype(BF16)
    direct_gather("mlp", y, NY, gtv, yag_ss.at[1], yag_rs.at[1])
    product = grad_scaled * normal
    gg_s[...] = jnp.sum(product.reshape(TY // 8, 8, DS), axis=0)

    def gain_x(o, carry):
        send(gg_s, ggx_r.at[o - 1], ggx_ss, ggx_rs, dp=lax.rem(x + o, NX))
        return carry
    lax.fori_loop(1, NX, gain_x, 0)
    join(1, gpx)

    arrived(ggx_r, ggx_rs)
    ggy_s[...] = gg_s[...] + jnp.sum(ggx_r[...], axis=0)

    def gain_y(o, carry):
        send(ggy_s, ggy_r.at[o - 1], ggy_ss, ggy_rs, mlp=lax.rem(y + o, NY))
        return carry
    lax.fori_loop(1, NY, gain_y, 0)

    end_x(1, scx)
    arrived(gpx.at[pl.ds(1, NX - 1), its_blocks], join_rs.at[1])
    product = dot(scx[...].reshape(NX * T, DS), gpx[...].reshape(NX * T, FQ), 0, 0)
    pieces = FQ // 128
    for j in range(pieces):
        gup[pl.ds(j, DS, stride=pieces), :] = product[:, j * 128 : (j + 1) * 128]
    arrived(outv.at[pl.ds(0, NY - 1)], yag_rs.at[0])
    out[...] = outv[...].reshape(T, DS)
    arrived(gtv.at[pl.ds(0, NY - 1)], yag_rs.at[1])
    gt[...] = gtv[...].reshape(T, DS)
    arrived(ggy_r, ggy_rs)
    gg[...] = jnp.sum(ggy_s[...] + jnp.sum(ggy_r[...], axis=0), axis=0)

    for k in range(2):
        arrived(sib_s.at[k], sib_ss.at[k])
        arrived(zs.at[k, pl.ds(0, NZ - 1)], z_ss.at[k])
    arrived(stat_r, stat_ss)
    for k, buf in enumerate((hid, gp)):
        arrived(buf.at[:, pl.ds(0, 5)], ag_ss.at[k])
        arrived(buf.at[0, pl.ds(0, 5)], rel_ss.at[k])
    for k, buf in enumerate((cotx, scx)):
        arrived(buf.at[pl.ds(0, NX - 1)], x_ss.at[k])
    for k, buf in enumerate((hx, gpx)):
        arrived(buf.at[pl.ds(1, NX - 1), my_blocks], q_ss.at[k])
        arrived(buf.at[pl.ds(1, NX - 1), my_blocks], join_ss.at[k])
    arrived(ys0.at[pl.ds(0, NY - 1)], y_ss.at[0])
    arrived(ys1.at[pl.ds(0, NY - 1)], y_ss.at[1])
    arrived(outv.at[pl.ds(0, NY - 1)], yag_ss.at[0])
    arrived(gtv.at[pl.ds(0, NY - 1)], yag_ss.at[1])
    arrived(ggx_r, ggx_ss)
    arrived(ggy_r, ggy_ss)


def place(*refs):
    made, given, sems = refs[0:5], refs[5:10], refs[10]
    copies = [pltpu.make_async_copy(src, dst, sems.at[k]) for k, (src, dst) in enumerate(zip(made, given))]
    for copy in copies:
        copy.start()
    for copy in copies:
        copy.wait()


def solution(mesh):
    NX, NZ, NY = mesh.shape["dp"], mesh.shape["width"] // 2, mesh.shape["mlp"]

    def shards(tokens, gain, up_weight, down_weight, cotangent):
        T, DS = tokens.shape
        FS = up_weight.shape[1]
        FH, FQ = FS // 2, FS // NX
        vmem, dma = pltpu.VMEM, pltpu.SemaphoreType.DMA
        results = (
            jax.ShapeDtypeStruct((T, DS), BF16),
            jax.ShapeDtypeStruct((T, DS), BF16),
            jax.ShapeDtypeStruct((DS,), F32),
            jax.ShapeDtypeStruct((DS * FQ // 128, 128), F32),
            jax.ShapeDtypeStruct((FQ, DS), F32),
        )
        call = pl.pallas_call(
            functools.partial(kernel, (NX, NZ, NY, DS * 2 * NZ)),
            out_shape=results,
            in_specs=[pl.BlockSpec(memory_space=pltpu.HBM)] * 5,
            out_specs=[pl.BlockSpec(memory_space=pltpu.VMEM)] * 5,
            scratch_shapes=[
                vmem((T, DS), BF16), vmem((DS,), F32), vmem((DS, FS), BF16), vmem((FS, DS), BF16),
                vmem((NX, T, DS), BF16), vmem((NX, T, DS), BF16), vmem((T, DS), F32), vmem((T, EXTRA), F32),
                vmem((2, 8, 128), F32), vmem((2 * NZ - 1, 8, 128), F32),
                vmem((2, T, FH), BF16), vmem((2, T, FH), BF16), vmem((2, NZ, TB, FH), F32),
                vmem((2, NZ, TB, FH), BF16), vmem((2, 6, TB, FH), BF16),
                vmem((2, 2, TB, FH // 2), BF16), vmem((2, 2, TB, FH), BF16),
                vmem((T + TB, DS), BF16), vmem((T, EXTRA), F32),
                vmem((2, NZ, TB, FH), BF16), vmem((2, NZ, TB, FH + EXTRA), BF16),
                vmem((NX, NZ, TB, FQ), BF16), vmem((NX, NZ, TB, FQ), BF16),
                *(
                    shape
                    for wide in (DS, DS + EXTRA)
                    for shape in (
                        vmem((NY, TB, wide), BF16), vmem((NY - 1, TB, wide), BF16), vmem((NY, TB, wide), F32),
                    )
                ),
                vmem((NY, TB, DS), BF16), vmem((NY, TB, DS), BF16),
                vmem((8, DS), F32), vmem((NX - 1, 8, DS), F32), vmem((8, DS), F32), vmem((NY - 1, 8, DS), F32),
                dma((5,)), dma((2,)), dma((2,)), dma, dma, dma((2,)), dma((2, 8)),
                dma((2,)), dma((2, 8)), dma((2, 4)), dma((2,)), dma((2,)),
                dma((2,)), dma((2, 4)), dma((2,)), dma((2,)), dma((2,)), dma((2,)),
                dma((2,)), dma((2,)), dma((2,)), dma((2,)), dma, dma, dma, dma,
            ],
            compiler_params=pltpu.CompilerParams(
                collective_id=0, has_side_effects=True, vmem_limit_bytes=48 * 1024 * 1024
            ),
            cost_estimate=pl.CostEstimate(
                flops=12 * T * DS * FS, bytes_accessed=4 * DS * FS + 8 * DS * FQ, transcendentals=2 * TB * FH
            ),
        )
        put = pl.pallas_call(
            place,
            out_shape=results,
            in_specs=[pl.BlockSpec(memory_space=pltpu.VMEM)] * 5,
            out_specs=[pl.BlockSpec(memory_space=pltpu.HBM)] * 5,
            scratch_shapes=[dma((5,))],
            compiler_params=pltpu.CompilerParams(vmem_limit_bytes=4 * 1024 * 1024),
        )
        output, grad_tokens, grad_gain, grad_up, grad_down = put(
            *call(*(pltpu.with_memory_space_constraint(a, pltpu.HBM) for a in (tokens, gain, up_weight, down_weight, cotangent)))
        )
        return output, grad_tokens, grad_gain, grad_up.reshape(DS, 1, FQ), grad_down[None, :, :]

    placed = (P("dp", "width"), P("width"), P("width", "mlp"), P("mlp", "width"), P("dp", "width"))
    return jax.shard_map(
        shards,
        mesh=mesh,
        in_specs=placed,
        out_specs=(
            P("dp", "width"),
            P("dp", "width"),
            P("width"),
            P("width", "mlp", "dp"),
            P("mlp", "dp", "width"),
        ),
        check_vma=False,
    )
```

time: 368 us -> 52.7 us (0.14)
  waiting for transfers between devices: 202 us -> 0 us
  blocking collectives: 131 us -> 0 us
  Pallas kernels: 0 us -> 51.8 us
  between operations: 13.9 us -> 0.64 us
  other arithmetic: 7.64 us -> 0 us
  matrix products: 7.63 us -> 0 us
  local copies, waits for them, and re-layouts: 4.66 us -> 0 us
    reduce_scatter x3 -> x0, waiting for transfers between devices: 136 us -> none  [the longest x1 61.3 us: shards(): lax.psum_scatter(contract(rows, down_weight, 1, 1).astype(jnp.bfloat16),...]
    psum x4 -> x0, blocking collectives: 95.4 us -> none  [the longest x1 30.6 us: shards(): token_sums = lax.psum(jnp.sum(inputs, axis=1), 'width')]
    psum x1 -> x0, waiting for transfers between devices: 66.3 us -> none  [shards(): output = lax.psum(partial_out.astype(jnp.bfloat16), 'mlp')]
    pallas_call x0 -> x2, Pallas kernels: none -> 51.8 us  [the longest x1 50.7 us: shards(): call(*(pltpu.with_memory_space_constraint(a, pltpu.HBM) for a in (tokens,...]
    all_gather x2 -> x0, blocking collectives: 35.8 us -> none  [the longest x1 18.6 us: shards(): grad_pre_all = lax.all_gather(grad_pre, 'width', axis=0, tiled=True)]
    dot_general x6 -> x0, matrix products: 7.63 us -> none  [the longest x4 4.54 us: contract(): lax.dot_general(left, right, (((left_dim,), (right_dim,)), ((), ())), pre...]
    unnamed x16 -> x0, local copies, waits for them, and re-layouts: 4.66 us -> none
  transfers between devices with their start and end apart: 5 -> 0, of which waited for: 4 -> 0; matrix products, arithmetic and copies ran while one was open for 3% -> 0% of each run, Pallas kernels for 0% -> 0%
where the time goes in v1:
time: 52.7 us; the launch traced here: 52.5 us
  Pallas kernels  51.8 us (98%)
  between operations  0.64 us (1%)
    pallas_call x1, Pallas kernels, shards(): call(*(pltpu.with_memory_space_constraint(a, pltpu.HBM) for a in (tokens,...  50.7 us
    pallas_call x1, Pallas kernels, shards(): put(*call(*(pltpu.with_memory_space_constraint(a, pltpu.HBM) for a in (to...  1.12 us

profile of v1, /device:TPU:1, one launch (start us, length us, event | category | flops | bytes accessed | tf_op | source)
XLA Modules:
  0.0 52.5 jit_solution(14054171499255930350)
XLA Ops:
  0.6 50.7 %shard_map.92 = (bf16[128,384]{1,0:T(8,128)(2,1)S(1)}, bf16[128,384]{1,0:T(8,128)(2,1)S(1)}, f32[384]{0:T(512)S(1)}, f32[1152,128]{1,0:T(8,128)S(1)}, f32[384,384]{1,0:T(8,128)S(1)}) custom-call(bf16[128,384]{1,0:T(8,128)(2,1)} %tok_h.1, f32[384]{0:T(512)} %gain_h.1, bf16[384,1536]{1,0:T(8,128)(2,1)} %wup_h.1, bf16[1536,384]{1,0:T(8,128)(2,1)} %wdn_h.1, ...), custom_call_target="tpu_custom_call" | custom-call | flops 905969664 | bytes 3538944 | tf_op jit(solution)/shard_map/pallas_call | solution.py:516
  51.3 1.1 %shard_map.93 = (bf16[128,384]{1,0:T(8,128)(2,1)}, bf16[128,384]{1,0:T(8,128)(2,1)}, f32[384]{0:T(512)}, f32[1152,128]{1,0:T(8,128)}, f32[384,384]{1,0:T(8,128)}) custom-call(bf16[128,384]{1,0:T(8,128)(2,1)S(1)} %get-tuple-element.15.refs_0_, bf16[128,384]{1,0:T(8,128)(2,1)S(1)} %get-tuple-element.16.refs_1_, f32[384]{0:T(512)S(1)} %get-tuple-element.17.refs_2_, ...), custom_call_target="tpu_custom_call" | custom-call | tf_op jit(solution)/shard_map/pallas_call | solution.py:515

commit v2 on v1

--- a/solution.py
+++ b/solution.py
@@ -368,48 +368,44 @@
         gp[1, :, :, 0:FH].reshape(T, FH), wup[:, FH:], 1, 1
     )
     side = (gp[0, :, :, FH:].astype(F32) + gp[1, :, :, FH:].astype(F32)).reshape(T, EXTRA)
-    part1[:, :, 0:DS] = term.reshape(NY, TY, DS)
-    ys1[:, :, 0:DS] = term.reshape(NY, TY, DS).astype(BF16)
-    part1[:, :, DS:] = side.reshape(NY, TY, EXTRA)
-    ys1[:, :, DS:] = pack(*unpack(side)).reshape(NY, TY, EXTRA)
+    first, second = unpack(side)
+    normal = normed[...]
+    corrected = inv_col[:, 0:1] * (
+        term * gain_v[...].reshape(1, DS) - first * (1.0 / D) - normal * (second * (1.0 / D))
+    )
+    corrected = corrected.reshape(NY, TY, DS)
+    part1[...] = corrected
+    ys1[...] = corrected.astype(BF16)
     direct_scatter("mlp", y, NY, ys1, yr1, y_ss.at[1], y_rs.at[1])
     share(1, gp, gpx)
+    gg_s[...] = jnp.sum((term * normal).reshape(T // 8, 8, DS), axis=0)
+
+    def gain_x(o, carry):
+        send(gg_s, ggx_r.at[o - 1], ggx_ss, ggx_rs, dp=lax.rem(x + o, NX))
+        return carry
+    lax.fori_loop(1, NX, gain_x, 0)
     pass_x(1, scx)
     join(0, hx)
 
     arrived(yr0, y_rs.at[0])
     outv[y] = (part0[y] + jnp.sum(yr0[...].astype(F32), axis=0)).astype(BF16)
     direct_gather("mlp", y, NY, outv, yag_ss.at[0], yag_rs.at[0])
+
+    arrived(ggx_r, ggx_rs)
+    ggy_s[...] = gg_s[...] + jnp.sum(ggx_r[...], axis=0)
+
+    def gain_y(o, carry):
+        send(ggy_s, ggy_r.at[o - 1], ggy_ss, ggy_rs, mlp=lax.rem(y + o, NY))
+        return carry
+    lax.fori_loop(1, NY, gain_y, 0)
 
     end_x(0, cotx)
     arrived(hx.at[pl.ds(1, NX - 1), its_blocks], join_rs.at[0])
     gdn[...] = dot(hx[...].reshape(NX * T, FQ), cotx[...].reshape(NX * T, DS), 0, 0)
     arrived(yr1, y_rs.at[1])
-    whole = part1[y] + jnp.sum(yr1[...].astype(F32), axis=0)
-    grad_scaled = whole[:, 0:DS]
-    first, second = unpack(whole[:, DS:])
-    block = pl.ds(pl.multiple_of(y * TY, TY), TY)
-    normal = normed[block, :]
-    gtv[y] = (
-        inv_col[block, 0:1] * (grad_scaled * gain_v[...].reshape(1, DS) - first * (1.0 / D) - normal * (second * (1.0 / D)))
-    ).astype(BF16)
+    gtv[y] = (part1[y] + jnp.sum(yr1[...].astype(F32), axis=0)).astype(BF16)
     direct_gather("mlp", y, NY, gtv, yag_ss.at[1], yag_rs.at[1])
-    product = grad_scaled * normal
-    gg_s[...] = jnp.sum(product.reshape(TY // 8, 8, DS), axis=0)
-
-    def gain_x(o, carry):
-        send(gg_s, ggx_r.at[o - 1], ggx_ss, ggx_rs, dp=lax.rem(x + o, NX))
-        return carry
-    lax.fori_loop(1, NX, gain_x, 0)
     join(1, gpx)
-
-    arrived(ggx_r, ggx_rs)
-    ggy_s[...] = gg_s[...] + jnp.sum(ggx_r[...], axis=0)
-
-    def gain_y(o, carry):
-        send(ggy_s, ggy_r.at[o - 1], ggy_ss, ggy_rs, mlp=lax.rem(y + o, NY))
-        return carry
-    lax.fori_loop(1, NY, gain_y, 0)
 
     end_x(1, scx)
     arrived(gpx.at[pl.ds(1, NX - 1), its_blocks], join_rs.at[1])
@@ -485,9 +481,9 @@
                 vmem((NX, NZ, TB, FQ), BF16), vmem((NX, NZ, TB, FQ), BF16),
                 *(
                     shape
-                    for wide in (DS, DS + EXTRA)
+                    for _ in range(2)
                     for shape in (
-                        vmem((NY, TB, wide), BF16), vmem((NY - 1, TB, wide), BF16), vmem((NY, TB, wide), F32),
+                        vmem((NY, TB, DS), BF16), vmem((NY - 1, TB, DS), BF16), vmem((NY, TB, DS), F32),
                     )
                 ),
                 vmem((NY, TB, DS), BF16), vmem((NY, TB, DS), BF16),

time: 52.7 us -> 51.7 us (0.981)
  Pallas kernels: 51.8 us -> 50.9 us
    pallas_call x1, Pallas kernels: 50.7 us -> 49.8 us  [shards(): call(*(pltpu.with_memory_space_constraint(a, pltpu.HBM) for a in (tokens,...]
where the time goes in v2:
time: 51.7 us; the launch traced here: 51.6 us
  Pallas kernels  50.9 us (98%)
  between operations  0.64 us (1%)
    pallas_call x1, Pallas kernels, shards(): call(*(pltpu.with_memory_space_constraint(a, pltpu.HBM) for a in (tokens,...  49.8 us
    pallas_call x1, Pallas kernels, shards(): put(*call(*(pltpu.with_memory_space_constraint(a, pltpu.HBM) for a in (to...  1.12 us

profile of v2, /device:TPU:1, one launch (start us, length us, event | category | flops | bytes accessed | tf_op | source)
XLA Modules:
  0.0 51.6 jit_solution(14273023295889066379)
XLA Ops:
  0.6 49.8 %shard_map.92 = (bf16[128,384]{1,0:T(8,128)(2,1)S(1)}, bf16[128,384]{1,0:T(8,128)(2,1)S(1)}, f32[384]{0:T(512)S(1)}, f32[1152,128]{1,0:T(8,128)S(1)}, f32[384,384]{1,0:T(8,128)S(1)}) custom-call(bf16[128,384]{1,0:T(8,128)(2,1)} %tok_h.1, f32[384]{0:T(512)} %gain_h.1, bf16[384,1536]{1,0:T(8,128)(2,1)} %wup_h.1, bf16[1536,384]{1,0:T(8,128)(2,1)} %wdn_h.1, ...), custom_call_target="tpu_custom_call" | custom-call | flops 905969664 | bytes 3538944 | tf_op jit(solution)/shard_map/pallas_call | solution.py:512
  50.5 1.1 %shard_map.93 = (bf16[128,384]{1,0:T(8,128)(2,1)}, bf16[128,384]{1,0:T(8,128)(2,1)}, f32[384]{0:T(512)}, f32[1152,128]{1,0:T(8,128)}, f32[384,384]{1,0:T(8,128)}) custom-call(bf16[128,384]{1,0:T(8,128)(2,1)S(1)} %get-tuple-element.15.refs_0_, bf16[128,384]{1,0:T(8,128)(2,1)S(1)} %get-tuple-element.16.refs_1_, f32[384]{0:T(512)S(1)} %get-tuple-element.17.refs_2_, ...), custom_call_target="tpu_custom_call" | custom-call | tf_op jit(solution)/shard_map/pallas_call | solution.py:511

commit v3 on v2

--- a/solution.py
+++ b/solution.py
@@ -121,27 +121,6 @@
         arrived(lanes_of(buf.at[at(4)], side), sems.at[first + 2 + side])
 
 
-def around(i, n):
-    half = lax.div(n - 2 - i, 2) + 1
-    return jnp.where(lax.rem(n - 2 - i, 2) == 0, half, n - half)
-
-
-def direct_scatter(axis, me, n, terms, got, ss, rs):
-    def one(i, carry):
-        o = around(i, n)
-        peer = lax.rem(me + o, n)
-        send(terms.at[peer], got.at[o - 1], ss, rs, **{axis: peer})
-        return carry
-    lax.fori_loop(0, n - 1, one, 0)
-
-
-def direct_gather(axis, me, n, buf, ss, rs):
-    def one(i, carry):
-        send(buf.at[me], buf.at[me], ss, rs, **{axis: lax.rem(me + around(i, n), n)})
-        return carry
-    lax.fori_loop(0, n - 1, one, 0)
-
-
 def kernel(
     sizes, tok_h, gain_h, wup_h, wdn_h, cot_h, out, gt, gg, gup, gdn,
     tok, gain_v, wup, wdn, cotx, scx, normed, inv_col,
@@ -150,7 +129,7 @@
     hid, gp, hx, gpx,
     ys0, yr0, part0, ys1, yr1, part1,
     outv, gtv,
-    gg_s, ggx_r, ggy_s, ggy_r,
+    gg_sum, gg_s, ggx_r, ggy_s, ggy_r,
     ld, sib_ss, sib_rs, stat_ss, stat_rs, z_ss, z_rs, ag_ss, ag_rs, far_rs, rel_ss, rel_rs,
     x_ss, x_rs, q_ss, q_rs, join_ss, join_rs, y_ss, y_rs, yag_ss, yag_rs, ggx_ss, ggx_rs, ggy_ss, ggy_rs,
 ):
@@ -298,6 +277,7 @@
         shift.append(functools.reduce(jnp.add, [my_aways[:, s : s + 1] * piece[s] for s in range(NW)]))
     lean_row = jnp.concatenate(leans, axis=1)
     shift = jnp.concatenate(shift, axis=1)
+
     def hand_over(k):
         return lambda block: send(block, block, rel_ss.at[k], rel_rs.at[k], width=sibling)
 
@@ -318,11 +298,6 @@
     gather(over_z, grads, ag_ss.at[1], ag_rs.at[1])
     hand_over(1)(gp.at[c, z])
 
-    gather_pass(over_z, across_z, units, ag_ss.at[0], ag_rs.at[0], far_rs.at[0], hand_over(0))
-    gather_near(over_z, units, ag_rs.at[0], hand_over(0))
-    gather_pass(over_z, across_z, grads, ag_ss.at[1], ag_rs.at[1], far_rs.at[1], hand_over(1))
-    gather_near(over_z, grads, ag_rs.at[1], hand_over(1))
-    pass_x(0, cotx)
     for j in range(DS // 128):
         cols = slice(j * 128, (j + 1) * 128)
         normal = (tok[:, cols].astype(F32) - mean_col) * std_col
@@ -330,18 +305,83 @@
         scx[0, :, cols] = (normal * g_all[:, cols]).astype(BF16)
     spread_x(1, scx)
 
-    def gathered(k, buf):
+    gather_pass(over_z, across_z, units, ag_ss.at[0], ag_rs.at[0], far_rs.at[0], hand_over(0))
+    gather_near(over_z, units, ag_rs.at[0], hand_over(0))
+    gather_pass(over_z, across_z, grads, ag_ss.at[1], ag_rs.at[1], far_rs.at[1], hand_over(1))
+    gather_near(over_z, grads, ag_rs.at[1], hand_over(1))
+    pass_x(0, cotx)
+
+    block_of, _ = over_z
+    near, far = (0, 1, -1, 2, -2), (3, -3, 4)
+
+    half_ring = NY // 2
+    slot = lax.rem(y, half_ring)
+
+    def next_to(o):
+        return lax.rem(y + o % NY, NY)
+
+    def own_sums(k, part, got, result):
+        arrived(got, y_rs.at[k])
+        for side in range(2):
+            block = lax.rem(y + side * half_ring, NY)
+            summed = part[block] + jnp.sum(got[side].astype(F32), axis=0)
+            result[lax.div(block, half_ring), lax.rem(block, half_ring)] = summed.astype(BF16)
+
+    def from_owners(k, buf):
+        both = buf.at[:, slot]
+        for side, o in ((0, 1), (1, -1)):
+            one = buf.at[side, slot]
+            send(one, one, yag_ss.at[k], yag_rs.at[k, 2 + side], mlp=next_to(2 * o))
+            send(both, both, yag_ss.at[k], yag_rs.at[k, side], mlp=next_to(o))
+
+    def from_owners_end(k, buf):
+        for side, o in ((0, -1), (1, 1)):
+            arrived(buf.at[:, lax.rem(next_to(o), half_ring)], yag_rs.at[k, side])
+            arrived(buf.at[side, lax.rem(next_to(2 * o), half_ring)], yag_rs.at[k, 2 + side])
+
+    def gathered_near(k, buf):
+        arrived(buf.at[1 - c, pl.ds(0, 5)], rel_rs.at[k])
+
+    def gathered_far(k, buf):
         gather_far(over_z, buf.at[c], ag_rs.at[k], 4)
         gather_far(over_z, buf.at[1 - c], far_rs.at[k], 0)
-        arrived(buf.at[1 - c, pl.ds(0, 5)], rel_rs.at[k])
-
-    gathered(0, hid)
-
-    term = dot(hid[0].reshape(T, FH), wdn[0:FH, :], 1, 0) + dot(hid[1].reshape(T, FH), wdn[FH:, :], 1, 0)
-    term = term.reshape(NY, TY, DS)
-    part0[...] = term
-    ys0[...] = term.astype(BF16)
-    direct_scatter("mlp", y, NY, ys0, yr0, y_ss.at[0], y_rs.at[0])
+
+    def rows_of(buf, h, blocks, lanes):
+        return jnp.concatenate([buf[h, block_of(o), :, lanes] for o in blocks], axis=0)
+
+    def to_owners(k, blocks, terms, part, sent, got):
+        for i, o in enumerate(blocks):
+            block = block_of(o)
+            part[block] = terms[i * TB : (i + 1) * TB]
+            sent[block] = terms[i * TB : (i + 1) * TB].astype(BF16)
+            for side in range(2):
+                owner = lax.rem(block + side * half_ring, NY)
+
+                @pl.when(owner != y)
+                def _():
+                    place_there = got.at[side, lax.rem(owner - y + NY - 1, NY)]
+                    send(sent.at[block], place_there, y_ss.at[k], y_rs.at[k], mlp=owner)
+
+    def output_terms(blocks):
+        units = slice(0, FH)
+        term = dot(rows_of(hid, 0, blocks, units), wdn[0:FH, :], 1, 0)
+        term = term + dot(rows_of(hid, 1, blocks, units), wdn[FH:, :], 1, 0)
+        to_owners(0, blocks, term, part0, ys0, yr0)
+
+    def gradient_terms(blocks):
+        units, beside = slice(0, FH), slice(FH, FH + EXTRA)
+        term = dot(rows_of(gp, 0, blocks, units), wup[:, 0:FH], 1, 1)
+        term = term + dot(rows_of(gp, 1, blocks, units), wup[:, FH:], 1, 1)
+        side = rows_of(gp, 0, blocks, beside).astype(F32) + rows_of(gp, 1, blocks, beside).astype(F32)
+        first, second = unpack(side)
+        tokens = [pl.ds(pl.multiple_of(block_of(o) * TB, TB), TB) for o in blocks]
+        normal = jnp.concatenate([normed[rows, :] for rows in tokens], axis=0)
+        scale = jnp.concatenate([inv_col[rows, 0:1] for rows in tokens], axis=0)
+        corrected = scale * (
+            term * gain_v[...].reshape(1, DS) - first * (1.0 / D) - normal * (second * (1.0 / D))
+        )
+        to_owners(1, blocks, corrected, part1, ys1, yr1)
+        return jnp.sum((term * normal).reshape(len(blocks) * TB // 8, 8, DS), axis=0)
 
     my_blocks = pl.ds(pl.multiple_of(c * (NZ // 2), NZ // 2), NZ // 2)
     its_blocks = pl.ds(pl.multiple_of((1 - c) * (NZ // 2), NZ // 2), NZ // 2)
@@ -361,24 +401,18 @@
         arrived(halves, q_rs.at[k])
         send(halves, halves, join_ss.at[k], join_rs.at[k], width=sibling)
 
+    gathered_near(0, hid)
+    output_terms(near)
+    gathered_near(1, gp)
+    gg_sum[...] = gradient_terms(near)
+    gathered_far(0, hid)
+    output_terms(far)
     share(0, hid, hx)
-
-    gathered(1, gp)
-    term = dot(gp[0, :, :, 0:FH].reshape(T, FH), wup[:, 0:FH], 1, 1) + dot(
-        gp[1, :, :, 0:FH].reshape(T, FH), wup[:, FH:], 1, 1
-    )
-    side = (gp[0, :, :, FH:].astype(F32) + gp[1, :, :, FH:].astype(F32)).reshape(T, EXTRA)
-    first, second = unpack(side)
-    normal = normed[...]
-    corrected = inv_col[:, 0:1] * (
-        term * gain_v[...].reshape(1, DS) - first * (1.0 / D) - normal * (second * (1.0 / D))
-    )
-    corrected = corrected.reshape(NY, TY, DS)
-    part1[...] = corrected
-    ys1[...] = corrected.astype(BF16)
-    direct_scatter("mlp", y, NY, ys1, yr1, y_ss.at[1], y_rs.at[1])
+    gathered_far(1, gp)
     share(1, gp, gpx)
-    gg_s[...] = jnp.sum((term * normal).reshape(T // 8, 8, DS), axis=0)
+    gains = jnp.sum(gg_sum[...] + gradient_terms(far), axis=0, keepdims=True)
+    rows = [gains[:, j * 128 : (j + 1) * 128] for j in range(DS // 128)]
+    gg_s[...] = jnp.concatenate(rows + [jnp.zeros((8 - len(rows), 128), F32)], axis=0)
 
     def gain_x(o, carry):
         send(gg_s, ggx_r.at[o - 1], ggx_ss, ggx_rs, dp=lax.rem(x + o, NX))
@@ -387,9 +421,8 @@
     pass_x(1, scx)
     join(0, hx)
 
-    arrived(yr0, y_rs.at[0])
-    outv[y] = (part0[y] + jnp.sum(yr0[...].astype(F32), axis=0)).astype(BF16)
-    direct_gather("mlp", y, NY, outv, yag_ss.at[0], yag_rs.at[0])
+    own_sums(0, part0, yr0, outv)
+    from_owners(0, outv)
 
     arrived(ggx_r, ggx_rs)
     ggy_s[...] = gg_s[...] + jnp.sum(ggx_r[...], axis=0)
@@ -399,26 +432,26 @@
         return carry
     lax.fori_loop(1, NY, gain_y, 0)
 
+    own_sums(1, part1, yr1, gtv)
+    from_owners(1, gtv)
+    join(1, gpx)
+
     end_x(0, cotx)
     arrived(hx.at[pl.ds(1, NX - 1), its_blocks], join_rs.at[0])
     gdn[...] = dot(hx[...].reshape(NX * T, FQ), cotx[...].reshape(NX * T, DS), 0, 0)
-    arrived(yr1, y_rs.at[1])
-    gtv[y] = (part1[y] + jnp.sum(yr1[...].astype(F32), axis=0)).astype(BF16)
-    direct_gather("mlp", y, NY, gtv, yag_ss.at[1], yag_rs.at[1])
-    join(1, gpx)
-
     end_x(1, scx)
     arrived(gpx.at[pl.ds(1, NX - 1), its_blocks], join_rs.at[1])
     product = dot(scx[...].reshape(NX * T, DS), gpx[...].reshape(NX * T, FQ), 0, 0)
     pieces = FQ // 128
     for j in range(pieces):
         gup[pl.ds(j, DS, stride=pieces), :] = product[:, j * 128 : (j + 1) * 128]
-    arrived(outv.at[pl.ds(0, NY - 1)], yag_rs.at[0])
+    from_owners_end(0, outv)
     out[...] = outv[...].reshape(T, DS)
-    arrived(gtv.at[pl.ds(0, NY - 1)], yag_rs.at[1])
+    from_owners_end(1, gtv)
     gt[...] = gtv[...].reshape(T, DS)
     arrived(ggy_r, ggy_rs)
-    gg[...] = jnp.sum(ggy_s[...] + jnp.sum(ggy_r[...], axis=0), axis=0)
+    gains = ggy_s[...] + jnp.sum(ggy_r[...], axis=0)
+    gg[...] = jnp.concatenate([gains[j : j + 1] for j in range(DS // 128)], axis=1).reshape(DS)
 
     for k in range(2):
         arrived(sib_s.at[k], sib_ss.at[k])
@@ -432,10 +465,10 @@
     for k, buf in enumerate((hx, gpx)):
         arrived(buf.at[pl.ds(1, NX - 1), my_blocks], q_ss.at[k])
         arrived(buf.at[pl.ds(1, NX - 1), my_blocks], join_ss.at[k])
-    arrived(ys0.at[pl.ds(0, NY - 1)], y_ss.at[0])
-    arrived(ys1.at[pl.ds(0, NY - 1)], y_ss.at[1])
-    arrived(outv.at[pl.ds(0, NY - 1)], yag_ss.at[0])
-    arrived(gtv.at[pl.ds(0, NY - 1)], yag_ss.at[1])
+    arrived(yr0, y_ss.at[0])
+    arrived(yr1, y_ss.at[1])
+    arrived(outv.at[:, pl.ds(0, 3)], yag_ss.at[0])
+    arrived(gtv.at[:, pl.ds(0, 3)], yag_ss.at[1])
     arrived(ggx_r, ggx_ss)
     arrived(ggy_r, ggy_ss)
 
@@ -483,15 +516,16 @@
                     shape
                     for _ in range(2)
                     for shape in (
-                        vmem((NY, TB, DS), BF16), vmem((NY - 1, TB, DS), BF16), vmem((NY, TB, DS), F32),
+                        vmem((NY, TB, DS), BF16), vmem((2, NY - 1, TB, DS), BF16), vmem((NY, TB, DS), F32),
                     )
                 ),
-                vmem((NY, TB, DS), BF16), vmem((NY, TB, DS), BF16),
-                vmem((8, DS), F32), vmem((NX - 1, 8, DS), F32), vmem((8, DS), F32), vmem((NY - 1, 8, DS), F32),
+                vmem((2, NY // 2, TB, DS), BF16), vmem((2, NY // 2, TB, DS), BF16),
+                vmem((8, DS), F32), vmem((8, 128), F32), vmem((NX - 1, 8, 128), F32),
+                vmem((8, 128), F32), vmem((NY - 1, 8, 128), F32),
                 dma((5,)), dma((2,)), dma((2,)), dma, dma, dma((2,)), dma((2, 8)),
                 dma((2,)), dma((2, 8)), dma((2, 4)), dma((2,)), dma((2,)),
                 dma((2,)), dma((2, 4)), dma((2,)), dma((2,)), dma((2,)), dma((2,)),
-                dma((2,)), dma((2,)), dma((2,)), dma((2,)), dma, dma, dma, dma,
+                dma((2,)), dma((2,)), dma((2,)), dma((2, 4)), dma, dma, dma, dma,
             ],
             compiler_params=pltpu.CompilerParams(
                 collective_id=0, has_side_effects=True, vmem_limit_bytes=48 * 1024 * 1024

time: 51.7 us -> 50.5 us (0.977); the launches traced: 51.6 us -> 49.6 us
  Pallas kernels: 50.9 us -> 48.9 us
    pallas_call x1, Pallas kernels: 49.8 us -> 47.8 us  [shards(): call(*(pltpu.with_memory_space_constraint(a, pltpu.HBM) for a in (tokens,...]
where the time goes in v3:
time: 50.5 us; the launch traced here: 49.6 us
  Pallas kernels  48.9 us (97%)
  between operations  0.64 us (1%)
    pallas_call x1, Pallas kernels, shards(): call(*(pltpu.with_memory_space_constraint(a, pltpu.HBM) for a in (tokens,...  47.8 us
    pallas_call x1, Pallas kernels, shards(): put(*call(*(pltpu.with_memory_space_constraint(a, pltpu.HBM) for a in (to...  1.12 us

profile of v3, /device:TPU:1, one launch (start us, length us, event | category | flops | bytes accessed | tf_op | source)
XLA Modules:
  0.0 49.6 jit_solution(15365815379814544658)
XLA Ops:
  0.6 47.8 %shard_map.92 = (bf16[128,384]{1,0:T(8,128)(2,1)S(1)}, bf16[128,384]{1,0:T(8,128)(2,1)S(1)}, f32[384]{0:T(512)S(1)}, f32[1152,128]{1,0:T(8,128)S(1)}, f32[384,384]{1,0:T(8,128)S(1)}) custom-call(bf16[128,384]{1,0:T(8,128)(2,1)} %tok_h.1, f32[384]{0:T(512)} %gain_h.1, bf16[384,1536]{1,0:T(8,128)(2,1)} %wup_h.1, bf16[1536,384]{1,0:T(8,128)(2,1)} %wdn_h.1, ...), custom_call_target="tpu_custom_call" | custom-call | flops 905969664 | bytes 3538944 | tf_op jit(solution)/shard_map/pallas_call | solution.py:546
  48.5 1.1 %shard_map.93 = (bf16[128,384]{1,0:T(8,128)(2,1)}, bf16[128,384]{1,0:T(8,128)(2,1)}, f32[384]{0:T(512)}, f32[1152,128]{1,0:T(8,128)}, f32[384,384]{1,0:T(8,128)}) custom-call(bf16[128,384]{1,0:T(8,128)(2,1)S(1)} %get-tuple-element.15.refs_0_, bf16[128,384]{1,0:T(8,128)(2,1)S(1)} %get-tuple-element.16.refs_1_, f32[384]{0:T(512)S(1)} %get-tuple-element.17.refs_2_, ...), custom_call_target="tpu_custom_call" | custom-call | tf_op jit(solution)/shard_map/pallas_call | solution.py:545

commit v4 on v3

--- a/solution.py
+++ b/solution.py
@@ -95,15 +95,15 @@
         send(block, block, ss, rs.at[slot], **to(o))
 
 
-def gather_pass(here, there, buf, ss, rs, far_rs, use):
+def gather_pass(here, buf, ss, sems, use):
     at, _ = here
     for side, o in ((0, 1), (1, -1)):
         block = buf.at[at(-2 * o)]
-        arrived(block, rs.at[2 + side])
+        arrived(block, sems[0][1].at[2 + side])
         half = lanes_of(block, side)
-        for (_, to), sems, first in ((here, rs, 4), (there, far_rs, 0)):
-            send(block, block, ss, sems.at[first + side], **to(o))
-            send(half, half, ss, sems.at[first + 2 + side], **to(2 * o))
+        for (_, to), there, first in sems:
+            send(block, block, ss, there.at[first + side], **to(o))
+            send(half, half, ss, there.at[first + 2 + side], **to(2 * o))
         use(block)
 
 
@@ -152,37 +152,40 @@
         h = lax.div(first, FH)
         return h, pl.ds(pl.multiple_of(first - h * FH, FQ), FQ)
 
+    mine = pl.ds(pl.multiple_of(c * FH, FH), FH)
+    other = pl.ds(pl.multiple_of(FH - c * FH, FH), FH)
+
+    barrier = pltpu.get_barrier_semaphore()
+
+    def greet(axis, me, n):
+        def one(i, carry):
+            step = lax.div(i + 1, 2)
+            o = n // 2 + jnp.where(lax.rem(i, 2) == 1, step, -step)
+            pl.semaphore_signal(barrier, inc=1, device_id={axis: lax.rem(me + o, n)}, device_id_type=MESH)
+            return carry
+        lax.fori_loop(0, n - 1, one, 0)
+
+    greet("mlp", y, NY)
+    greet("width", w, NW)
+    greet("dp", x, NX)
+
     loads = [
         pltpu.make_async_copy(tok_h, tok, ld.at[0]),
         pltpu.make_async_copy(gain_h, gain_v, ld.at[1]),
-        pltpu.make_async_copy(wup_h, wup, ld.at[2]),
+        pltpu.make_async_copy(wup_h.at[:, other], wup.at[:, other], ld.at[2]),
         pltpu.make_async_copy(cot_h, cotx.at[0], ld.at[3]),
-        pltpu.make_async_copy(wdn_h, wdn, ld.at[4]),
+        pltpu.make_async_copy(wdn_h.at[other], wdn.at[other], ld.at[4]),
+        pltpu.make_async_copy(wup_h.at[:, mine], wup.at[:, mine], ld.at[5]),
+        pltpu.make_async_copy(wdn_h.at[mine], wdn.at[mine], ld.at[6]),
     ]
     for load in loads:
         load.start()
-
-    barrier = pltpu.get_barrier_semaphore()
-
-    def greet(axis, me, n):
-        def one(k, carry):
-            pl.semaphore_signal(barrier, inc=1, device_id={axis: lax.rem(me + k, n)}, device_id_type=MESH)
-            return carry
-        lax.fori_loop(1, n, one, 0)
-
-    greet("width", w, NW)
-    greet("mlp", y, NY)
-    greet("dp", x, NX)
-
-    mine = pl.ds(pl.multiple_of(c * FH, FH), FH)
-    other = pl.ds(pl.multiple_of(FH - c * FH, FH), FH)
 
     loads[0].wait()
     loads[1].wait()
     values = tok[...].astype(F32)
     total = jnp.sum(values, axis=1, keepdims=True)
     shifted = values - total * (1.0 / DS)
-    spread = jnp.sum(shifted * shifted, axis=1, keepdims=True)
     g_all = gain_v[...].reshape(1, DS)
     leaning[0:T] = (shifted * g_all).astype(BF16)
     row = lax.broadcasted_iota(jnp.int32, (TB, DS), 0)
@@ -193,30 +196,18 @@
     loads[2].wait()
     its_half = dot(leaning[...], wup[:, other], 1, 0)
     sib_s[0] = its_half[0:T].astype(BF16)
-    pl.semaphore_wait(barrier, NW - 1 + NY - 1 + NX - 1)
-    send(sib_s.at[0], sib_r.at[0], sib_ss.at[0], sib_rs.at[0], width=sibling)
 
     loads[3].wait()
     loads[4].wait()
     sib_s[1] = dot(cotx[0], wdn[other, :], 1, 1).astype(BF16)
-    send(sib_s.at[1], sib_r.at[1], sib_ss.at[1], sib_rs.at[1], width=sibling)
-
-    def merge(k, mine_half):
-        arrived(sib_r.at[k], sib_rs.at[k])
-        both = (mine_half + sib_r[k].astype(F32)).reshape(NZ, TB, FH)
-        own[k] = both
-        zs[k] = both.astype(BF16)
-        scatter(over_z, zs.at[k], zr.at[k], [zh.at[k, 0], zh.at[k, 1]], z_ss.at[k], z_rs.at[k])
-
-    def merge_pass(k):
-        scatter_pass(
-            over_z, own.at[k], zr.at[k], [zh.at[k, 0], zh.at[k, 1]], zc.at[k], z_ss.at[k], z_rs.at[k]
-        )
-
+    loads[5].wait()
     my_half = dot(leaning[...], wup[:, mine], 1, 0)
-    merge(0, my_half[0:T])
-    merge(1, dot(cotx[0], wdn[mine, :], 1, 1))
-
+    own[0] = my_half[0:T].reshape(NZ, TB, FH)
+    loads[6].wait()
+    own[1] = dot(cotx[0], wdn[mine, :], 1, 1).reshape(NZ, TB, FH)
+
+    shifted = tok[...].astype(F32) - total * (1.0 / DS)
+    spread = jnp.sum(shifted * shifted, axis=1, keepdims=True)
     total_row = jnp.transpose(jnp.broadcast_to(total, (T, EXTRA)))[0:1]
     spread_row = jnp.transpose(jnp.broadcast_to(spread, (T, EXTRA)))[0:1]
     for h, half in ((c, my_half), (1 - c, its_half)):
@@ -226,12 +217,31 @@
         for j in range(FH // 128):
             stat_s[h, 2 + j : 3 + j, :] = lean[:, j * 128 : (j + 1) * 128]
 
+    pl.semaphore_wait(barrier, NW - 1 + NY - 1 + NX - 1)
+    for k in range(2):
+        send(sib_s.at[k], sib_r.at[k], sib_ss.at[k], sib_rs.at[k], width=sibling)
+
     def tell(k, carry):
         peer = lax.rem(w + k, NW)
         send(stat_s.at[lax.rem(peer, 2)], stat_r.at[k - 1], stat_ss, stat_rs, width=peer)
         return carry
     lax.fori_loop(1, NW, tell, 0)
 
+    def merge(k):
+        arrived(sib_r.at[k], sib_rs.at[k])
+        both = own[k] + sib_r[k].astype(F32).reshape(NZ, TB, FH)
+        own[k] = both
+        zs[k] = both.astype(BF16)
+        scatter(over_z, zs.at[k], zr.at[k], [zh.at[k, 0], zh.at[k, 1]], z_ss.at[k], z_rs.at[k])
+
+    def merge_pass(k):
+        scatter_pass(
+            over_z, own.at[k], zr.at[k], [zh.at[k, 0], zh.at[k, 1]], zc.at[k], z_ss.at[k], z_rs.at[k]
+        )
+
+    merge(0)
+    merge(1)
+
     right, left = lax.rem(x + 1, NX), lax.rem(x + NX - 1, NX)
     first_rows, last_rows = pl.ds(0, T // 2), pl.ds(T // 2, T // 2)
 
@@ -249,9 +259,9 @@
         arrived(buf.at[2, first_rows], x_rs.at[k, 2])
         arrived(buf.at[2, last_rows], x_rs.at[k, 3])
 
+    spread_x(0, cotx)
     merge_pass(0)
     merge_pass(1)
-    spread_x(0, cotx)
 
     arrived(stat_r, stat_rs)
     its = stat_r[...]
@@ -305,9 +315,11 @@
         scx[0, :, cols] = (normal * g_all[:, cols]).astype(BF16)
     spread_x(1, scx)
 
-    gather_pass(over_z, across_z, units, ag_ss.at[0], ag_rs.at[0], far_rs.at[0], hand_over(0))
+    gather_pass(over_z, units, ag_ss.at[0], [(over_z, ag_rs.at[0], 4)], hand_over(0))
     gather_near(over_z, units, ag_rs.at[0], hand_over(0))
-    gather_pass(over_z, across_z, grads, ag_ss.at[1], ag_rs.at[1], far_rs.at[1], hand_over(1))
+    gather_pass(
+        over_z, grads, ag_ss.at[1], [(over_z, ag_rs.at[1], 4), (across_z, far_rs, 0)], hand_over(1)
+    )
     gather_near(over_z, grads, ag_rs.at[1], hand_over(1))
     pass_x(0, cotx)
 
@@ -338,13 +350,6 @@
         for side, o in ((0, -1), (1, 1)):
             arrived(buf.at[:, lax.rem(next_to(o), half_ring)], yag_rs.at[k, side])
             arrived(buf.at[side, lax.rem(next_to(2 * o), half_ring)], yag_rs.at[k, 2 + side])
-
-    def gathered_near(k, buf):
-        arrived(buf.at[1 - c, pl.ds(0, 5)], rel_rs.at[k])
-
-    def gathered_far(k, buf):
-        gather_far(over_z, buf.at[c], ag_rs.at[k], 4)
-        gather_far(over_z, buf.at[1 - c], far_rs.at[k], 0)
 
     def rows_of(buf, h, blocks, lanes):
         return jnp.concatenate([buf[h, block_of(o), :, lanes] for o in blocks], axis=0)
@@ -401,16 +406,22 @@
         arrived(halves, q_rs.at[k])
         send(halves, halves, join_ss.at[k], join_rs.at[k], width=sibling)
 
-    gathered_near(0, hid)
+    arrived(hid.at[1 - c, pl.ds(0, 5)], rel_rs.at[0])
     output_terms(near)
-    gathered_near(1, gp)
+    gather_far(over_z, units, ag_rs.at[0], 4)
+    for o in far:
+        block = hid.at[c, block_of(o)]
+        send(block, block, rel_ss.at[0], rel_rs.at[2], width=sibling)
+    arrived(gp.at[1 - c, pl.ds(0, 5)], rel_rs.at[1])
     gg_sum[...] = gradient_terms(near)
-    gathered_far(0, hid)
+    arrived(hid.at[1 - c, pl.ds(0, 3)], rel_rs.at[2])
     output_terms(far)
     share(0, hid, hx)
-    gathered_far(1, gp)
+    gather_far(over_z, grads, ag_rs.at[1], 4)
+    gather_far(over_z, gp.at[1 - c], far_rs, 0)
+    gains = gg_sum[...] + gradient_terms(far)
     share(1, gp, gpx)
-    gains = jnp.sum(gg_sum[...] + gradient_terms(far), axis=0, keepdims=True)
+    gains = jnp.sum(gains, axis=0, keepdims=True)
     rows = [gains[:, j * 128 : (j + 1) * 128] for j in range(DS // 128)]
     gg_s[...] = jnp.concatenate(rows + [jnp.zeros((8 - len(rows), 128), F32)], axis=0)
 
@@ -432,34 +443,27 @@
         return carry
     lax.fori_loop(1, NY, gain_y, 0)
 
-    own_sums(1, part1, yr1, gtv)
-    from_owners(1, gtv)
     join(1, gpx)
 
     end_x(0, cotx)
     arrived(hx.at[pl.ds(1, NX - 1), its_blocks], join_rs.at[0])
     gdn[...] = dot(hx[...].reshape(NX * T, FQ), cotx[...].reshape(NX * T, DS), 0, 0)
+    own_sums(1, part1, yr1, gtv)
+    from_owners(1, gtv)
     end_x(1, scx)
     arrived(gpx.at[pl.ds(1, NX - 1), its_blocks], join_rs.at[1])
     product = dot(scx[...].reshape(NX * T, DS), gpx[...].reshape(NX * T, FQ), 0, 0)
     pieces = FQ // 128
     for j in range(pieces):
         gup[pl.ds(j, DS, stride=pieces), :] = product[:, j * 128 : (j + 1) * 128]
-    from_owners_end(0, outv)
-    out[...] = outv[...].reshape(T, DS)
-    from_owners_end(1, gtv)
-    gt[...] = gtv[...].reshape(T, DS)
-    arrived(ggy_r, ggy_rs)
-    gains = ggy_s[...] + jnp.sum(ggy_r[...], axis=0)
-    gg[...] = jnp.concatenate([gains[j : j + 1] for j in range(DS // 128)], axis=1).reshape(DS)
-
     for k in range(2):
         arrived(sib_s.at[k], sib_ss.at[k])
         arrived(zs.at[k, pl.ds(0, NZ - 1)], z_ss.at[k])
     arrived(stat_r, stat_ss)
-    for k, buf in enumerate((hid, gp)):
-        arrived(buf.at[:, pl.ds(0, 5)], ag_ss.at[k])
-        arrived(buf.at[0, pl.ds(0, 5)], rel_ss.at[k])
+    arrived(hid.at[0, pl.ds(0, NZ - 1)], ag_ss.at[0])
+    arrived(hid.at[0], rel_ss.at[0])
+    arrived(gp.at[:, pl.ds(0, 5)], ag_ss.at[1])
+    arrived(gp.at[0, pl.ds(0, 5)], rel_ss.at[1])
     for k, buf in enumerate((cotx, scx)):
         arrived(buf.at[pl.ds(0, NX - 1)], x_ss.at[k])
     for k, buf in enumerate((hx, gpx)):
@@ -468,8 +472,16 @@
     arrived(yr0, y_ss.at[0])
     arrived(yr1, y_ss.at[1])
     arrived(outv.at[:, pl.ds(0, 3)], yag_ss.at[0])
+    arrived(ggx_r, ggx_ss)
+
+    from_owners_end(0, outv)
+    out[...] = outv[...].reshape(T, DS)
+    from_owners_end(1, gtv)
+    gt[...] = gtv[...].reshape(T, DS)
+    arrived(ggy_r, ggy_rs)
+    gains = ggy_s[...] + jnp.sum(ggy_r[...], axis=0)
+    gg[...] = jnp.concatenate([gains[j : j + 1] for j in range(DS // 128)], axis=1).reshape(DS)
     arrived(gtv.at[:, pl.ds(0, 3)], yag_ss.at[1])
-    arrived(ggx_r, ggx_ss)
     arrived(ggy_r, ggy_ss)
 
 
@@ -522,8 +534,8 @@
                 vmem((2, NY // 2, TB, DS), BF16), vmem((2, NY // 2, TB, DS), BF16),
                 vmem((8, DS), F32), vmem((8, 128), F32), vmem((NX - 1, 8, 128), F32),
                 vmem((8, 128), F32), vmem((NY - 1, 8, 128), F32),
-                dma((5,)), dma((2,)), dma((2,)), dma, dma, dma((2,)), dma((2, 8)),
-                dma((2,)), dma((2, 8)), dma((2, 4)), dma((2,)), dma((2,)),
+                dma((7,)), dma((2,)), dma((2,)), dma, dma, dma((2,)), dma((2, 8)),
+                dma((2,)), dma((2, 8)), dma((4,)), dma((2,)), dma((3,)),
                 dma((2,)), dma((2, 4)), dma((2,)), dma((2,)), dma((2,)), dma((2,)),
                 dma((2,)), dma((2,)), dma((2,)), dma((2, 4)), dma, dma, dma, dma,
             ],

time: 50.5 us -> 49.6 us (0.982); the launches traced: 49.6 us -> 49.4 us
  no operation moved by 1% of the time
where the time goes in v4:
time: 49.6 us; the launch traced here: 49.4 us
  Pallas kernels  48.7 us (98%)
  between operations  0.64 us (1%)
    pallas_call x1, Pallas kernels, shards(): call(*(pltpu.with_memory_space_constraint(a, pltpu.HBM) for a in (tokens,...  47.6 us
    pallas_call x1, Pallas kernels, shards(): put(*call(*(pltpu.with_memory_space_constraint(a, pltpu.HBM) for a in (to...  1.12 us

profile of v4, /device:TPU:1, one launch (start us, length us, event | category | flops | bytes accessed | tf_op | source)
XLA Modules:
  0.0 49.4 jit_solution(4402113490651090463)
XLA Ops:
  0.6 47.6 %shard_map.92 = (bf16[128,384]{1,0:T(8,128)(2,1)S(1)}, bf16[128,384]{1,0:T(8,128)(2,1)S(1)}, f32[384]{0:T(512)S(1)}, f32[1152,128]{1,0:T(8,128)S(1)}, f32[384,384]{1,0:T(8,128)S(1)}) custom-call(bf16[128,384]{1,0:T(8,128)(2,1)} %tok_h.1, f32[384]{0:T(512)} %gain_h.1, bf16[384,1536]{1,0:T(8,128)(2,1)} %wup_h.1, bf16[1536,384]{1,0:T(8,128)(2,1)} %wdn_h.1, ...), custom_call_target="tpu_custom_call" | custom-call | flops 905969664 | bytes 3538944 | tf_op jit(solution)/shard_map/pallas_call | solution.py:558
  48.2 1.1 %shard_map.93 = (bf16[128,384]{1,0:T(8,128)(2,1)}, bf16[128,384]{1,0:T(8,128)(2,1)}, f32[384]{0:T(512)}, f32[1152,128]{1,0:T(8,128)}, f32[384,384]{1,0:T(8,128)}) custom-call(bf16[128,384]{1,0:T(8,128)(2,1)S(1)} %get-tuple-element.15.refs_0_, bf16[128,384]{1,0:T(8,128)(2,1)S(1)} %get-tuple-element.16.refs_1_, f32[384]{0:T(512)S(1)} %get-tuple-element.17.refs_2_, ...), custom_call_target="tpu_custom_call" | custom-call | tf_op jit(solution)/shard_map/pallas_call | solution.py:557

commit v5 on v4

--- a/solution.py
+++ b/solution.py
@@ -132,6 +132,7 @@
     gg_sum, gg_s, ggx_r, ggy_s, ggy_r,
     ld, sib_ss, sib_rs, stat_ss, stat_rs, z_ss, z_rs, ag_ss, ag_rs, far_rs, rel_ss, rel_rs,
     x_ss, x_rs, q_ss, q_rs, join_ss, join_rs, y_ss, y_rs, yag_ss, yag_rs, ggx_ss, ggx_rs, ggy_ss, ggy_rs,
+    known, all_known,
 ):
     NX, NZ, NY, D = sizes
     T, DS = tok.shape
@@ -156,18 +157,17 @@
     other = pl.ds(pl.multiple_of(FH - c * FH, FH), FH)
 
     barrier = pltpu.get_barrier_semaphore()
-
-    def greet(axis, me, n):
-        def one(i, carry):
-            step = lax.div(i + 1, 2)
-            o = n // 2 + jnp.where(lax.rem(i, 2) == 1, step, -step)
-            pl.semaphore_signal(barrier, inc=1, device_id={axis: lax.rem(me + o, n)}, device_id_type=MESH)
-            return carry
-        lax.fori_loop(0, n - 1, one, 0)
-
-    greet("mlp", y, NY)
-    greet("width", w, NW)
-    greet("dp", x, NX)
+    over_y = ring("mlp", y)
+
+    def signal(semaphore, **where):
+        pl.semaphore_signal(semaphore, inc=1, device_id=where, device_id_type=MESH)
+
+    for o in (2, -2, 1, -1):
+        signal(barrier, **over_z[1](o))
+        signal(barrier, **over_y[1](o))
+    for o in range(1, NX):
+        signal(barrier, dp=lax.rem(x + o, NX))
+    signal(barrier, width=sibling)
 
     loads = [
         pltpu.make_async_copy(tok_h, tok, ld.at[0]),
@@ -200,6 +200,14 @@
     loads[3].wait()
     loads[4].wait()
     sib_s[1] = dot(cotx[0], wdn[other, :], 1, 1).astype(BF16)
+    pl.semaphore_wait(barrier, 8 + NX)
+    for k in range(2):
+        send(sib_s.at[k], sib_r.at[k], sib_ss.at[k], sib_rs.at[k], width=sibling)
+    signal(known, width=sibling)
+    for o in (2, -2):
+        signal(known, **over_z[1](o))
+        signal(known, **over_y[1](o))
+
     loads[5].wait()
     my_half = dot(leaning[...], wup[:, mine], 1, 0)
     own[0] = my_half[0:T].reshape(NZ, TB, FH)
@@ -217,16 +225,6 @@
         for j in range(FH // 128):
             stat_s[h, 2 + j : 3 + j, :] = lean[:, j * 128 : (j + 1) * 128]
 
-    pl.semaphore_wait(barrier, NW - 1 + NY - 1 + NX - 1)
-    for k in range(2):
-        send(sib_s.at[k], sib_r.at[k], sib_ss.at[k], sib_rs.at[k], width=sibling)
-
-    def tell(k, carry):
-        peer = lax.rem(w + k, NW)
-        send(stat_s.at[lax.rem(peer, 2)], stat_r.at[k - 1], stat_ss, stat_rs, width=peer)
-        return carry
-    lax.fori_loop(1, NW, tell, 0)
-
     def merge(k):
         arrived(sib_r.at[k], sib_rs.at[k])
         both = own[k] + sib_r[k].astype(F32).reshape(NZ, TB, FH)
@@ -239,8 +237,17 @@
             over_z, own.at[k], zr.at[k], [zh.at[k, 0], zh.at[k, 1]], zc.at[k], z_ss.at[k], z_rs.at[k]
         )
 
+    def tell(k, carry):
+        peer = lax.rem(w + k, NW)
+        send(stat_s.at[lax.rem(peer, 2)], stat_r.at[k - 1], stat_ss, stat_rs, width=peer)
+        return carry
+
     merge(0)
+    pl.semaphore_wait(known, 5)
+    signal(all_known, width=sibling)
     merge(1)
+    pl.semaphore_wait(all_known, 1)
+    lax.fori_loop(1, NW, tell, 0)
 
     right, left = lax.rem(x + 1, NX), lax.rem(x + NX - 1, NX)
     first_rows, last_rows = pl.ds(0, T // 2), pl.ds(T // 2, T // 2)
@@ -538,6 +545,7 @@
                 dma((2,)), dma((2, 8)), dma((4,)), dma((2,)), dma((3,)),
                 dma((2,)), dma((2, 4)), dma((2,)), dma((2,)), dma((2,)), dma((2,)),
                 dma((2,)), dma((2,)), dma((2,)), dma((2, 4)), dma, dma, dma, dma,
+                pltpu.SemaphoreType.REGULAR, pltpu.SemaphoreType.REGULAR,
             ],
             compiler_params=pltpu.CompilerParams(
                 collective_id=0, has_side_effects=True, vmem_limit_bytes=48 * 1024 * 1024

time: 49.6 us -> 48.7 us (0.982)
  Pallas kernels: 48.7 us -> 47.9 us
    pallas_call x1, Pallas kernels: 47.6 us -> 46.8 us  [shards(): call(*(pltpu.with_memory_space_constraint(a, pltpu.HBM) for a in (tokens,...]
where the time goes in v5:
time: 48.7 us; the launch traced here: 48.5 us
  Pallas kernels  47.9 us (98%)
  between operations  0.64 us (1%)
    pallas_call x1, Pallas kernels, shards(): call(*(pltpu.with_memory_space_constraint(a, pltpu.HBM) for a in (tokens,...  46.8 us
    pallas_call x1, Pallas kernels, shards(): put(*call(*(pltpu.with_memory_space_constraint(a, pltpu.HBM) for a in (to...  1.12 us

profile of v5, /device:TPU:1, one launch (start us, length us, event | category | flops | bytes accessed | tf_op | source)
XLA Modules:
  0.0 48.5 jit_solution(10521597394135596461)
XLA Ops:
  0.6 46.8 %shard_map.92 = (bf16[128,384]{1,0:T(8,128)(2,1)S(1)}, bf16[128,384]{1,0:T(8,128)(2,1)S(1)}, f32[384]{0:T(512)S(1)}, f32[1152,128]{1,0:T(8,128)S(1)}, f32[384,384]{1,0:T(8,128)S(1)}) custom-call(bf16[128,384]{1,0:T(8,128)(2,1)} %tok_h.1, f32[384]{0:T(512)} %gain_h.1, bf16[384,1536]{1,0:T(8,128)(2,1)} %wup_h.1, bf16[1536,384]{1,0:T(8,128)(2,1)} %wdn_h.1, ...), custom_call_target="tpu_custom_call" | custom-call | flops 905969664 | bytes 3538944 | tf_op jit(solution)/shard_map/pallas_call | solution.py:566
  47.4 1.1 %shard_map.93 = (bf16[128,384]{1,0:T(8,128)(2,1)}, bf16[128,384]{1,0:T(8,128)(2,1)}, f32[384]{0:T(512)}, f32[1152,128]{1,0:T(8,128)}, f32[384,384]{1,0:T(8,128)}) custom-call(bf16[128,384]{1,0:T(8,128)(2,1)S(1)} %get-tuple-element.15.refs_0_, bf16[128,384]{1,0:T(8,128)(2,1)S(1)} %get-tuple-element.16.refs_1_, f32[384]{0:T(512)S(1)} %get-tuple-element.17.refs_2_, ...), custom_call_target="tpu_custom_call" | custom-call | tf_op jit(solution)/shard_map/pallas_call | solution.py:565

commit v6 on v5

--- a/solution.py
+++ b/solution.py
@@ -197,17 +197,17 @@
     its_half = dot(leaning[...], wup[:, other], 1, 0)
     sib_s[0] = its_half[0:T].astype(BF16)
 
-    loads[3].wait()
-    loads[4].wait()
-    sib_s[1] = dot(cotx[0], wdn[other, :], 1, 1).astype(BF16)
     pl.semaphore_wait(barrier, 8 + NX)
-    for k in range(2):
-        send(sib_s.at[k], sib_r.at[k], sib_ss.at[k], sib_rs.at[k], width=sibling)
+    send(sib_s.at[0], sib_r.at[0], sib_ss.at[0], sib_rs.at[0], width=sibling)
     signal(known, width=sibling)
     for o in (2, -2):
         signal(known, **over_z[1](o))
         signal(known, **over_y[1](o))
 
+    loads[3].wait()
+    loads[4].wait()
+    sib_s[1] = dot(cotx[0], wdn[other, :], 1, 1).astype(BF16)
+    send(sib_s.at[1], sib_r.at[1], sib_ss.at[1], sib_rs.at[1], width=sibling)
     loads[5].wait()
     my_half = dot(leaning[...], wup[:, mine], 1, 0)
     own[0] = my_half[0:T].reshape(NZ, TB, FH)
@@ -423,10 +423,10 @@
     gg_sum[...] = gradient_terms(near)
     arrived(hid.at[1 - c, pl.ds(0, 3)], rel_rs.at[2])
     output_terms(far)
-    share(0, hid, hx)
     gather_far(over_z, grads, ag_rs.at[1], 4)
     gather_far(over_z, gp.at[1 - c], far_rs, 0)
     gains = gg_sum[...] + gradient_terms(far)
+    share(0, hid, hx)
     share(1, gp, gpx)
     gains = jnp.sum(gains, axis=0, keepdims=True)
     rows = [gains[:, j * 128 : (j + 1) * 128] for j in range(DS // 128)]
@@ -450,13 +450,12 @@
         return carry
     lax.fori_loop(1, NY, gain_y, 0)
 
-    join(1, gpx)
-
     end_x(0, cotx)
     arrived(hx.at[pl.ds(1, NX - 1), its_blocks], join_rs.at[0])
     gdn[...] = dot(hx[...].reshape(NX * T, FQ), cotx[...].reshape(NX * T, DS), 0, 0)
     own_sums(1, part1, yr1, gtv)
     from_owners(1, gtv)
+    join(1, gpx)
     end_x(1, scx)
     arrived(gpx.at[pl.ds(1, NX - 1), its_blocks], join_rs.at[1])
     product = dot(scx[...].reshape(NX * T, DS), gpx[...].reshape(NX * T, FQ), 0, 0)

time: 48.7 us -> 50.7 us (1.041)
  Pallas kernels: 47.9 us -> 50 us
    pallas_call x1, Pallas kernels: 46.8 us -> 48.8 us  [shards(): call(*(pltpu.with_memory_space_constraint(a, pltpu.HBM) for a in (tokens,...]
where the time goes in v6:
time: 50.7 us; the launch traced here: 50.6 us
  Pallas kernels  50 us (99%)
  between operations  0.64 us (1%)
    pallas_call x1, Pallas kernels, shards(): call(*(pltpu.with_memory_space_constraint(a, pltpu.HBM) for a in (tokens,...  48.8 us
    pallas_call x1, Pallas kernels, shards(): put(*call(*(pltpu.with_memory_space_constraint(a, pltpu.HBM) for a in (to...  1.12 us

profile of v6, /device:TPU:1, one launch (start us, length us, event | category | flops | bytes accessed | tf_op | source)
XLA Modules:
  0.0 50.6 jit_solution(11364732217838237483)
XLA Ops:
  0.6 48.8 %shard_map.92 = (bf16[128,384]{1,0:T(8,128)(2,1)S(1)}, bf16[128,384]{1,0:T(8,128)(2,1)S(1)}, f32[384]{0:T(512)S(1)}, f32[1152,128]{1,0:T(8,128)S(1)}, f32[384,384]{1,0:T(8,128)S(1)}) custom-call(bf16[128,384]{1,0:T(8,128)(2,1)} %tok_h.1, f32[384]{0:T(512)} %gain_h.1, bf16[384,1536]{1,0:T(8,128)(2,1)} %wup_h.1, bf16[1536,384]{1,0:T(8,128)(2,1)} %wdn_h.1, ...), custom_call_target="tpu_custom_call" | custom-call | flops 905969664 | bytes 3538944 | tf_op jit(solution)/shard_map/pallas_call | solution.py:565
  49.5 1.1 %shard_map.93 = (bf16[128,384]{1,0:T(8,128)(2,1)}, bf16[128,384]{1,0:T(8,128)(2,1)}, f32[384]{0:T(512)}, f32[1152,128]{1,0:T(8,128)}, f32[384,384]{1,0:T(8,128)}) custom-call(bf16[128,384]{1,0:T(8,128)(2,1)S(1)} %get-tuple-element.15.refs_0_, bf16[128,384]{1,0:T(8,128)(2,1)S(1)} %get-tuple-element.16.refs_1_, f32[384]{0:T(512)S(1)} %get-tuple-element.17.refs_2_, ...), custom_call_target="tpu_custom_call" | custom-call | tf_op jit(solution)/shard_map/pallas_call | solution.py:564

commit v7 on v5

--- a/solution.py
+++ b/solution.py
@@ -329,6 +329,7 @@
     )
     gather_near(over_z, grads, ag_rs.at[1], hand_over(1))
     pass_x(0, cotx)
+    pass_x(1, scx)
 
     block_of, _ = over_z
     near, far = (0, 1, -1, 2, -2), (3, -3, 4)
@@ -426,8 +427,8 @@
     share(0, hid, hx)
     gather_far(over_z, grads, ag_rs.at[1], 4)
     gather_far(over_z, gp.at[1 - c], far_rs, 0)
+    share(1, gp, gpx)
     gains = gg_sum[...] + gradient_terms(far)
-    share(1, gp, gpx)
     gains = jnp.sum(gains, axis=0, keepdims=True)
     rows = [gains[:, j * 128 : (j + 1) * 128] for j in range(DS // 128)]
     gg_s[...] = jnp.concatenate(rows + [jnp.zeros((8 - len(rows), 128), F32)], axis=0)
@@ -436,7 +437,6 @@
         send(gg_s, ggx_r.at[o - 1], ggx_ss, ggx_rs, dp=lax.rem(x + o, NX))
         return carry
     lax.fori_loop(1, NX, gain_x, 0)
-    pass_x(1, scx)
     join(0, hx)
 
     own_sums(0, part0, yr0, outv)

time: 48.7 us -> 48.7 us (level)
  no operation moved by 1% of the time
where the time goes in v7:
time: 48.7 us; the launch traced here: 48.5 us
  Pallas kernels  47.9 us (98%)
  between operations  0.64 us (1%)
    pallas_call x1, Pallas kernels, shards(): call(*(pltpu.with_memory_space_constraint(a, pltpu.HBM) for a in (tokens,...  46.8 us
    pallas_call x1, Pallas kernels, shards(): put(*call(*(pltpu.with_memory_space_constraint(a, pltpu.HBM) for a in (to...  1.12 us

profile of v7, /device:TPU:1, one launch (start us, length us, event | category | flops | bytes accessed | tf_op | source)
XLA Modules:
  0.0 48.5 jit_solution(16126640966771553888)
XLA Ops:
  0.6 46.8 %shard_map.92 = (bf16[128,384]{1,0:T(8,128)(2,1)S(1)}, bf16[128,384]{1,0:T(8,128)(2,1)S(1)}, f32[384]{0:T(512)S(1)}, f32[1152,128]{1,0:T(8,128)S(1)}, f32[384,384]{1,0:T(8,128)S(1)}) custom-call(bf16[128,384]{1,0:T(8,128)(2,1)} %tok_h.1, f32[384]{0:T(512)} %gain_h.1, bf16[384,1536]{1,0:T(8,128)(2,1)} %wup_h.1, bf16[1536,384]{1,0:T(8,128)(2,1)} %wdn_h.1, ...), custom_call_target="tpu_custom_call" | custom-call | flops 905969664 | bytes 3538944 | tf_op jit(solution)/shard_map/pallas_call | solution.py:566
  47.4 1.1 %shard_map.93 = (bf16[128,384]{1,0:T(8,128)(2,1)}, bf16[128,384]{1,0:T(8,128)(2,1)}, f32[384]{0:T(512)}, f32[1152,128]{1,0:T(8,128)}, f32[384,384]{1,0:T(8,128)}) custom-call(bf16[128,384]{1,0:T(8,128)(2,1)S(1)} %get-tuple-element.15.refs_0_, bf16[128,384]{1,0:T(8,128)(2,1)S(1)} %get-tuple-element.16.refs_1_, f32[384]{0:T(512)S(1)} %get-tuple-element.17.refs_2_, ...), custom_call_target="tpu_custom_call" | custom-call | tf_op jit(solution)/shard_map/pallas_call | solution.py:565

commit v8 on v6

--- a/solution.py
+++ b/solution.py
@@ -329,6 +329,7 @@
     )
     gather_near(over_z, grads, ag_rs.at[1], hand_over(1))
     pass_x(0, cotx)
+    pass_x(1, scx)
 
     block_of, _ = over_z
     near, far = (0, 1, -1, 2, -2), (3, -3, 4)
@@ -423,11 +424,11 @@
     gg_sum[...] = gradient_terms(near)
     arrived(hid.at[1 - c, pl.ds(0, 3)], rel_rs.at[2])
     output_terms(far)
+    share(0, hid, hx)
     gather_far(over_z, grads, ag_rs.at[1], 4)
     gather_far(over_z, gp.at[1 - c], far_rs, 0)
+    share(1, gp, gpx)
     gains = gg_sum[...] + gradient_terms(far)
-    share(0, hid, hx)
-    share(1, gp, gpx)
     gains = jnp.sum(gains, axis=0, keepdims=True)
     rows = [gains[:, j * 128 : (j + 1) * 128] for j in range(DS // 128)]
     gg_s[...] = jnp.concatenate(rows + [jnp.zeros((8 - len(rows), 128), F32)], axis=0)
@@ -436,7 +437,6 @@
         send(gg_s, ggx_r.at[o - 1], ggx_ss, ggx_rs, dp=lax.rem(x + o, NX))
         return carry
     lax.fori_loop(1, NX, gain_x, 0)
-    pass_x(1, scx)
     join(0, hx)
 
     own_sums(0, part0, yr0, outv)
@@ -449,13 +449,14 @@
         send(ggy_s, ggy_r.at[o - 1], ggy_ss, ggy_rs, mlp=lax.rem(y + o, NY))
         return carry
     lax.fori_loop(1, NY, gain_y, 0)
+
+    join(1, gpx)
 
     end_x(0, cotx)
     arrived(hx.at[pl.ds(1, NX - 1), its_blocks], join_rs.at[0])
     gdn[...] = dot(hx[...].reshape(NX * T, FQ), cotx[...].reshape(NX * T, DS), 0, 0)
     own_sums(1, part1, yr1, gtv)
     from_owners(1, gtv)
-    join(1, gpx)
     end_x(1, scx)
     arrived(gpx.at[pl.ds(1, NX - 1), its_blocks], join_rs.at[1])
     product = dot(scx[...].reshape(NX * T, DS), gpx[...].reshape(NX * T, FQ), 0, 0)

time: 50.7 us -> 50 us (0.986)
  Pallas kernels: 50 us -> 49.3 us
    pallas_call x1, Pallas kernels: 48.8 us -> 48.1 us  [shards(): call(*(pltpu.with_memory_space_constraint(a, pltpu.HBM) for a in (tokens,...]
where the time goes in v8:
time: 50 us; the launch traced here: 49.9 us
  Pallas kernels  49.3 us (99%)
  between operations  0.64 us (1%)
    pallas_call x1, Pallas kernels, shards(): call(*(pltpu.with_memory_space_constraint(a, pltpu.HBM) for a in (tokens,...  48.1 us
    pallas_call x1, Pallas kernels, shards(): put(*call(*(pltpu.with_memory_space_constraint(a, pltpu.HBM) for a in (to...  1.12 us

profile of v8, /device:TPU:1, one launch (start us, length us, event | category | flops | bytes accessed | tf_op | source)
XLA Modules:
  0.0 49.9 jit_solution(17006843002440090736)
XLA Ops:
  0.6 48.1 %shard_map.92 = (bf16[128,384]{1,0:T(8,128)(2,1)S(1)}, bf16[128,384]{1,0:T(8,128)(2,1)S(1)}, f32[384]{0:T(512)S(1)}, f32[1152,128]{1,0:T(8,128)S(1)}, f32[384,384]{1,0:T(8,128)S(1)}) custom-call(bf16[128,384]{1,0:T(8,128)(2,1)} %tok_h.1, f32[384]{0:T(512)} %gain_h.1, bf16[384,1536]{1,0:T(8,128)(2,1)} %wup_h.1, bf16[1536,384]{1,0:T(8,128)(2,1)} %wdn_h.1, ...), custom_call_target="tpu_custom_call" | custom-call | flops 905969664 | bytes 3538944 | tf_op jit(solution)/shard_map/pallas_call | solution.py:566
  48.8 1.1 %shard_map.93 = (bf16[128,384]{1,0:T(8,128)(2,1)}, bf16[128,384]{1,0:T(8,128)(2,1)}, f32[384]{0:T(512)}, f32[1152,128]{1,0:T(8,128)}, f32[384,384]{1,0:T(8,128)}) custom-call(bf16[128,384]{1,0:T(8,128)(2,1)S(1)} %get-tuple-element.15.refs_0_, bf16[128,384]{1,0:T(8,128)(2,1)S(1)} %get-tuple-element.16.refs_1_, f32[384]{0:T(512)S(1)} %get-tuple-element.17.refs_2_, ...), custom_call_target="tpu_custom_call" | custom-call | tf_op jit(solution)/shard_map/pallas_call | solution.py:565

commit v9 on v7

--- a/solution.py
+++ b/solution.py
@@ -243,11 +243,9 @@
         return carry
 
     merge(0)
+    merge(1)
     pl.semaphore_wait(known, 5)
     signal(all_known, width=sibling)
-    merge(1)
-    pl.semaphore_wait(all_known, 1)
-    lax.fori_loop(1, NW, tell, 0)
 
     right, left = lax.rem(x + 1, NX), lax.rem(x + NX - 1, NX)
     first_rows, last_rows = pl.ds(0, T // 2), pl.ds(T // 2, T // 2)
@@ -267,6 +265,8 @@
         arrived(buf.at[2, last_rows], x_rs.at[k, 3])
 
     spread_x(0, cotx)
+    pl.semaphore_wait(all_known, 1)
+    lax.fori_loop(1, NW, tell, 0)
     merge_pass(0)
     merge_pass(1)
 

time: 48.7 us -> 49 us (level)
  no operation moved by 1% of the time
where the time goes in v9:
time: 49 us; the launch traced here: 48.8 us
  Pallas kernels  48.2 us (98%)
  between operations  0.64 us (1%)
    pallas_call x1, Pallas kernels, shards(): call(*(pltpu.with_memory_space_constraint(a, pltpu.HBM) for a in (tokens,...  47.1 us
    pallas_call x1, Pallas kernels, shards(): put(*call(*(pltpu.with_memory_space_constraint(a, pltpu.HBM) for a in (to...  1.12 us

profile of v9, /device:TPU:1, one launch (start us, length us, event | category | flops | bytes accessed | tf_op | source)
XLA Modules:
  0.0 48.8 jit_solution(5872810850733344236)
XLA Ops:
  0.6 47.1 %shard_map.92 = (bf16[128,384]{1,0:T(8,128)(2,1)S(1)}, bf16[128,384]{1,0:T(8,128)(2,1)S(1)}, f32[384]{0:T(512)S(1)}, f32[1152,128]{1,0:T(8,128)S(1)}, f32[384,384]{1,0:T(8,128)S(1)}) custom-call(bf16[128,384]{1,0:T(8,128)(2,1)} %tok_h.1, f32[384]{0:T(512)} %gain_h.1, bf16[384,1536]{1,0:T(8,128)(2,1)} %wup_h.1, bf16[1536,384]{1,0:T(8,128)(2,1)} %wdn_h.1, ...), custom_call_target="tpu_custom_call" | custom-call | flops 905969664 | bytes 3538944 | tf_op jit(solution)/shard_map/pallas_call | solution.py:566
  47.7 1.1 %shard_map.93 = (bf16[128,384]{1,0:T(8,128)(2,1)}, bf16[128,384]{1,0:T(8,128)(2,1)}, f32[384]{0:T(512)}, f32[1152,128]{1,0:T(8,128)}, f32[384,384]{1,0:T(8,128)}) custom-call(bf16[128,384]{1,0:T(8,128)(2,1)S(1)} %get-tuple-element.15.refs_0_, bf16[128,384]{1,0:T(8,128)(2,1)S(1)} %get-tuple-element.16.refs_1_, f32[384]{0:T(512)S(1)} %get-tuple-element.17.refs_2_, ...), custom_call_target="tpu_custom_call" | custom-call | tf_op jit(solution)/shard_map/pallas_call | solution.py:565

commit v10 on v9

--- a/solution.py
+++ b/solution.py
@@ -328,8 +328,6 @@
         over_z, grads, ag_ss.at[1], [(over_z, ag_rs.at[1], 4), (across_z, far_rs, 0)], hand_over(1)
     )
     gather_near(over_z, grads, ag_rs.at[1], hand_over(1))
-    pass_x(0, cotx)
-    pass_x(1, scx)
 
     block_of, _ = over_z
     near, far = (0, 1, -1, 2, -2), (3, -3, 4)
@@ -422,6 +420,8 @@
         send(block, block, rel_ss.at[0], rel_rs.at[2], width=sibling)
     arrived(gp.at[1 - c, pl.ds(0, 5)], rel_rs.at[1])
     gg_sum[...] = gradient_terms(near)
+    pass_x(0, cotx)
+    pass_x(1, scx)
     arrived(hid.at[1 - c, pl.ds(0, 3)], rel_rs.at[2])
     output_terms(far)
     share(0, hid, hx)

time: 49 us -> 48.7 us (level)
  Pallas kernels: 48.2 us -> 47.7 us
    pallas_call x1, Pallas kernels: 47.1 us -> 46.6 us  [shards(): call(*(pltpu.with_memory_space_constraint(a, pltpu.HBM) for a in (tokens,...]
where the time goes in v10:
time: 48.7 us; the launch traced here: 48.3 us
  Pallas kernels  47.7 us (98%)
  between operations  0.64 us (1%)
    pallas_call x1, Pallas kernels, shards(): call(*(pltpu.with_memory_space_constraint(a, pltpu.HBM) for a in (tokens,...  46.6 us
    pallas_call x1, Pallas kernels, shards(): put(*call(*(pltpu.with_memory_space_constraint(a, pltpu.HBM) for a in (to...  1.12 us

profile of v10, /device:TPU:1, one launch (start us, length us, event | category | flops | bytes accessed | tf_op | source)
XLA Modules:
  0.0 48.3 jit_solution(10590772840285412893)
XLA Ops:
  0.6 46.6 %shard_map.92 = (bf16[128,384]{1,0:T(8,128)(2,1)S(1)}, bf16[128,384]{1,0:T(8,128)(2,1)S(1)}, f32[384]{0:T(512)S(1)}, f32[1152,128]{1,0:T(8,128)S(1)}, f32[384,384]{1,0:T(8,128)S(1)}) custom-call(bf16[128,384]{1,0:T(8,128)(2,1)} %tok_h.1, f32[384]{0:T(512)} %gain_h.1, bf16[384,1536]{1,0:T(8,128)(2,1)} %wup_h.1, bf16[1536,384]{1,0:T(8,128)(2,1)} %wdn_h.1, ...), custom_call_target="tpu_custom_call" | custom-call | flops 905969664 | bytes 3538944 | tf_op jit(solution)/shard_map/pallas_call | solution.py:566
  47.2 1.1 %shard_map.93 = (bf16[128,384]{1,0:T(8,128)(2,1)}, bf16[128,384]{1,0:T(8,128)(2,1)}, f32[384]{0:T(512)}, f32[1152,128]{1,0:T(8,128)}, f32[384,384]{1,0:T(8,128)}) custom-call(bf16[128,384]{1,0:T(8,128)(2,1)S(1)} %get-tuple-element.15.refs_0_, bf16[128,384]{1,0:T(8,128)(2,1)S(1)} %get-tuple-element.16.refs_1_, f32[384]{0:T(512)S(1)} %get-tuple-element.17.refs_2_, ...), custom_call_target="tpu_custom_call" | custom-call | tf_op jit(solution)/shard_map/pallas_call | solution.py:565
